TPU v7x, 32 devices: a whole 2x2x4 slice. The times are simulated.
32 devices in a mesh: slab: 2 (over core), vel: 16 (over z, y, x).
Axes of the slice: x: 2, y: 2, z: 4, core: 2. Of those that a mesh axis runs over, the one named last changes fastest.
Arguments:
- f_start: float32 [4096, 2, 8, 128], P('vel', 'slab'), as said below
- links: int32 [3, 2, 8, 128], P(None, 'slab'), may hold values 0 or 1
- solid: int32 [2, 8, 128], P('slab'), may hold values 0 or 1
Outputs:
- f_final: float32 [4096, 2, 8, 128], P('vel', 'slab')
Inputs may be any that keep to these rules, and one draw needn't show every extreme that they name: `f_start`: every entry is positive.
All inputs are finite; a program needn't handle non-finite values. No bound on the sum of `links` or of `solid` on one device may be relied on, other than what follows from the above.
Results may differ from a plain program's by a relative error of at most 0.0003.
Values sent between devices are 32-bit elements; how exact they have to be, the bound alone decides.
A program may use at most 64 MiB of HBM per device.

v0:
```python
import math

import jax
import jax.numpy as jnp
from jax import lax
from jax.sharding import PartitionSpec as P

NQ = 16
STEPS = 2
SWEEPS = 2


SPACING = 0.6
COUPLING = 1.0
COURANT = 0.06
RELAXATION_FREQ = 0.5
VISCOUS_TO_HEAT = 2.0 / 3.0
QUAD_WEIGHT = SPACING**3 / (2.0 * math.pi) ** 1.5


def passed_along(block, axis, distance):
    devices = range(lax.axis_size(axis))
    route = [(i - distance, i) for i in devices if i - distance in devices]
    return lax.ppermute(block, axis, route)


def padded_2(cells, sides, width):
    for axis, dim in sides:
        count = lax.axis_size(axis)
        ends = count - 1
        head = lax.slice_in_dim(cells, 0, width, axis=dim)
        tail = lax.slice_in_dim(cells, cells.shape[dim] - width, cells.shape[dim], axis=dim)
        cells = jnp.concatenate(
            [
                lax.ppermute(tail, axis, [(i, (i + 1) % count) for i in range(ends)]),
                cells,
                lax.ppermute(head, axis, [((i + 1) % count, i) for i in range(ends)]),
            ],
            axis=dim,
        )
    return cells


def lattice_of(first, number):
    index = first + lax.iota(jnp.int32, number)
    comp_x = index % NQ
    comp_y = index // NQ % NQ
    comp_z = index // (NQ * NQ)
    stacked = jnp.stack([comp_x, comp_y, comp_z]).astype(jnp.float32)
    return (stacked - (NQ - 1) / 2.0) * SPACING


def moment_basis(lattice):
    overall_work_content = 0.5 * jnp.sum(lattice * lattice, axis=0)
    rows = [
        jnp.ones_like(overall_work_content),
        lattice[0],
        lattice[1],
        lattice[2],
        overall_work_content,
        lattice[0] * overall_work_content,
        lattice[1] * overall_work_content,
        lattice[2] * overall_work_content,
    ]
    return jnp.stack(rows) * QUAD_WEIGHT


def shift_down(values, axis_dim):
    pads = [(0, 0)] * values.ndim
    pads[axis_dim] = (1, 0)
    return lax.slice_in_dim(jnp.pad(values, pads), 0, values.shape[axis_dim], axis=axis_dim)


def shift_up(values, axis_dim):
    pads = [(0, 0)] * values.ndim
    pads[axis_dim] = (0, 1)
    return lax.slice_in_dim(jnp.pad(values, pads), 1, values.shape[axis_dim] + 1, axis=axis_dim)


def macro_state(predicted):
    matter_per_volume = predicted[0]
    mean_flow_vector = predicted[1:4] / matter_per_volume
    overall_work_content = predicted[4]
    fluid_hotness_level = (
        2.0 * overall_work_content / matter_per_volume
        - jnp.sum(mean_flow_vector * mean_flow_vector, axis=0)
    ) / 3.0
    fluid_normal_stress = matter_per_volume * fluid_hotness_level
    heat_current_vector = predicted[5:8] - mean_flow_vector * (
        overall_work_content + fluid_normal_stress
    )
    relaxation_update = RELAXATION_FREQ * matter_per_volume * fluid_hotness_level**0.28
    profile_multiplier = (
        (1.0 - VISCOUS_TO_HEAT)
        * heat_current_vector
        / (5.0 * fluid_normal_stress * fluid_hotness_level)
    )
    perturbation_height = matter_per_volume * fluid_hotness_level ** (-1.5)
    return (
        mean_flow_vector,
        fluid_hotness_level,
        relaxation_update,
        profile_multiplier,
        perturbation_height,
    )


def upwind_local(dist, speed, axis_dim):
    return jnp.where(speed > 0, shift_down(dist, axis_dim), shift_up(dist, axis_dim))


def transport(dist, upwind_x, lattice, particle_population, open_up, open_low, solid):
    (
        mean_flow_vector,
        fluid_hotness_level,
        relaxation_update,
        profile_multiplier,
        perturbation_height,
    ) = particle_population
    peculiar = lattice[:, :, None, None, None] - mean_flow_vector[:, None]
    acoustic_celerity_power = jnp.sum(peculiar * peculiar, axis=0)
    matching_arrangement = jnp.sum(peculiar * profile_multiplier[:, None], axis=0)
    relaxed_distribution_goal = (
        perturbation_height
        * jnp.exp(-acoustic_celerity_power / (2.0 * fluid_hotness_level))
        * (1.0 + matching_arrangement * (acoustic_celerity_power / fluid_hotness_level - 5.0))
    )
    flux = jnp.zeros_like(dist)
    for axis_dim in range(3):
        speed = lattice[axis_dim][:, None, None, None]
        rising = speed > 0
        outward = jnp.where(rising, open_up[axis_dim], open_low[axis_dim])
        inward = jnp.where(rising, open_low[axis_dim], open_up[axis_dim])
        if axis_dim == 0:
            neighbour = upwind_x
        else:
            neighbour = upwind_local(dist, speed, axis_dim + 1)
        flux = flux + jnp.abs(speed) * (outward * dist - inward * neighbour)
    fresh = (dist - COURANT * flux + relaxation_update * relaxed_distribution_goal) / (
        1.0 + relaxation_update
    )
    return jnp.where(solid > 0, dist, fresh)


def relax(moments, padded, open_up, open_low, count):
    center = padded[:, 1:-1, :, 1:-1]
    beside_all = (
        padded[:, 2:, :, 1:-1] * open_up[0]
        + padded[:, :-2, :, 1:-1] * open_low[0]
        + shift_up(center, 2) * open_up[1]
        + shift_down(center, 2) * open_low[1]
        + padded[:, 1:-1, :, 2:] * open_up[2]
        + padded[:, 1:-1, :, :-2] * open_low[2]
    )
    return (moments + COUPLING * beside_all) / (1.0 + COUPLING * count)


def body(f_start, links, solid):
    vel_local = f_start.shape[0]
    rank = lax.axis_index("vel")
    lattice = lattice_of(rank * vel_local, vel_local)
    basis = moment_basis(lattice)
    open_up = links.astype(jnp.float32)
    plane = passed_along(links[0, -1:], "slab", 1)
    low_x = jnp.concatenate([plane, links[0, :-1]], axis=0).astype(jnp.float32)
    open_low = jnp.stack([low_x, shift_down(open_up[1], 1), shift_down(open_up[2], 2)])
    count = jnp.sum(open_up, axis=0) + jnp.sum(open_low, axis=0)
    dist = f_start
    for repeat in range(STEPS):
        partial_value = jnp.dot(basis, dist.reshape(vel_local, -1), precision=lax.Precision.HIGHEST)
        partial_value = partial_value.reshape((8,) + dist.shape[1:])
        moments = lax.psum(partial_value, "vel")
        predicted = moments
        for sweeping in range(SWEEPS):
            padded = padded_2(predicted, (("slab", 1),), 1)
            padded = jnp.pad(padded, ((0, 0), (0, 0), (0, 0), (1, 1)))
            predicted = relax(moments, padded, open_up, open_low, count)
        particle_population = macro_state(predicted)
        extended = padded_2(dist, (("slab", 1),), 1)
        speed = lattice[0][:, None, None, None]
        upwind_x = jnp.where(speed > 0, extended[:, :-2], extended[:, 2:])
        dist = transport(dist, upwind_x, lattice, particle_population, open_up, open_low, solid)
    return dist


def solution(mesh):
    in_specs = (P("vel", "slab", None, None), P(None, "slab", None, None), P("slab", None, None))
    out_specs = P("vel", "slab", None, None)
    return jax.shard_map(body, mesh=mesh, in_specs=in_specs, out_specs=out_specs, check_vma=False)
```

profile of v0, /device:TPU:1, one launch (start us, length us, event | category | flops | bytes accessed | tf_op | source)
XLA Modules:
  0.0 195.0 jit_solution(11182977201358130271)
XLA Ops:
  0.1 1.4 copy.33
  1.5 0.3 copy.20
  1.8 0.0 copy-start
  1.9 0.0 copy-start.1
  1.9 0.0 copy-start.2
  1.9 1.0 convolution_bitcast_fusion.1
  2.9 63.7 %psum.14 = f32[8,1,8,128]{3,0,2,1:T(8,128)S(1)} all-reduce(f32[8,1,8,128]{3,0,2,1:T(8,128)S(1)} %convolution_bitcast_fusion.1), channel_id=1, replica_groups=mesh['slab'=2,'vel'=16] {'vel'}, use_global_device_ids=true, to_apply=%region_1.2 | all-reduce | flops 8192 | bytes 65536 | tf_op jit(solution)/shard_map/psum | solution.py:172
  66.6 1.3 collective-permute-start.4
  67.9 16.8 %collective-permute-start.3 = (f32[8,1,8,128]{3,0,2,1:T(8,128)S(1)}, f32[8,1,8,128]{3,0,2,1:T(8,128)S(1)}, u32[]{:S(2)}, u32[]{:S(2)}) collective-permute-start(f32[8,1,8,128]{3,0,2,1:T(8,128)S(1)} %psum.14), channel_id=1, source_target_pairs={{16,0},{17,1},{18,2},{19,3},{20,4},{21,5},{22,6},{23,7},{24,8},{25... | collective-permute-start | bytes 98312 | tf_op jit(solution)/shard_map/ppermute | solution.py:37
  84.7 0.0 copy-done
  84.7 1.3 collective-permute-start.1
  86.0 3.2 %collective-permute-start.2 = (f32[256,1,8,128]{3,2,0,1:T(8,128)S(1)}, f32[256,1,8,128]{3,2,0,1:T(8,128)S(1)}, u32[]{:S(2)}, u32[]{:S(2)}) collective-permute-start(f32[256,1,8,128]{3,2,0,1:T(8,128)S(1)} %bitcast.158), channel_id=1, source_target_pairs={{16,0},{17,1},{18,2},{19,3},{20,4},{21,5},{22,6},{23,7},{24,8},{25... | collective-permute-start | bytes 3145736 | tf_op jit(solution)/shard_map/ppermute | solution.py:37
  89.2 0.0 copy-done.1
  89.2 1.3 collective-permute-start
  90.5 0.0 copy-done.2
  90.6 0.1 fusion.92
  90.7 1.6 collective-permute-done
  92.3 0.1 add_add_fusion
  92.4 0.0 collective-permute-done.4
  92.4 0.0 collective-permute-done.3
  92.4 0.1 select_maximum_fusion.6
  92.5 0.1 fusion.56
  92.6 1.3 collective-permute-start.6
  93.9 3.0 %collective-permute-start.5 = (f32[8,1,8,128]{3,0,2,1:T(8,128)S(1)}, f32[8,1,8,128]{3,0,2,1:T(8,128)S(1)}, u32[]{:S(2)}, u32[]{:S(2)}) collective-permute-start(f32[8,1,8,128]{3,0,2,1:T(8,128)S(1)} %fusion.56), channel_id=1, source_target_pairs={{16,0},{17,1},{18,2},{19,3},{20,4},{21,5},{22,6},{23,7},{24,8},{25... | collective-permute-start | bytes 98312 | tf_op jit(solution)/shard_map/ppermute | solution.py:37
  96.9 0.0 collective-permute-done.6
  97.0 0.8 collective-permute-done.5
  97.8 0.1 select_maximum_fusion.4
  97.9 0.1 fusion.64
  98.1 1.1 fusion
  99.3 0.0 collective-permute-done.1
  99.3 0.0 collective-permute-done.2
  99.3 3.1 %fusion.12 = f32[256,1,8,128]{3,2,0,1:T(8,128)S(1)} fusion(f32[256,1,8,128]{3,2,0,1:T(8,128)S(1)} %bitcast.159, f32[256,8,128]{2,1,0:T(8,128)S(1)} %get-tuple-element.8, f32[256,8,128]{2,1,0:T(8,128)S(1)} %get-tuple-element.7, f32[256,1,8,128]{3,2,0,1:T(8,128)S(1)} %collective-permute-done.1, f32[256,1,8,128]{3,2,0,1:T(8,128)S(1)} %collective-permute-done.2, ...), kind=kLoop, calls=%fused_computation.38 | loop fusion | flops 9699328 | bytes 6341376 | tf_op jit(solution)/shard_map/jit(_where)/select_n | solution.py:142
  102.4 0.2 copy.32
  102.6 0.3 copy.24
  103.0 1.0 convolution_bitcast_fusion
  103.9 57.8 %psum.15 = f32[8,1,8,128]{3,0,2,1:T(8,128)S(1)} all-reduce(f32[8,1,8,128]{3,0,2,1:T(8,128)S(1)} %convolution_bitcast_fusion), channel_id=1, replica_groups=mesh['slab'=2,'vel'=16] {'vel'}, use_global_device_ids=true, to_apply=%region_6.7 | all-reduce | flops 8192 | bytes 65536 | tf_op jit(solution)/shard_map/psum | solution.py:172
  161.8 1.3 collective-permute-start.10
  163.1 16.2 %collective-permute-start.9 = (f32[8,1,8,128]{3,0,2,1:T(8,128)S(1)}, f32[8,1,8,128]{3,0,2,1:T(8,128)S(1)}, u32[]{:S(2)}, u32[]{:S(2)}) collective-permute-start(f32[8,1,8,128]{3,0,2,1:T(8,128)S(1)} %psum.15), channel_id=1, source_target_pairs={{16,0},{17,1},{18,2},{19,3},{20,4},{21,5},{22,6},{23,7},{24,8},{25... | collective-permute-start | bytes 98312 | tf_op jit(solution)/shard_map/ppermute | solution.py:37
  179.2 0.0 collective-permute-done.10
  179.2 0.8 collective-permute-done.9
  180.1 0.1 select_maximum_fusion.2
  180.2 0.1 fusion.72
  180.3 1.3 collective-permute-start.12
  181.6 3.0 %collective-permute-start.11 = (f32[8,1,8,128]{3,0,2,1:T(8,128)S(1)}, f32[8,1,8,128]{3,0,2,1:T(8,128)S(1)}, u32[]{:S(2)}, u32[]{:S(2)}) collective-permute-start(f32[8,1,8,128]{3,0,2,1:T(8,128)S(1)} %fusion.72), channel_id=1, source_target_pairs={{16,0},{17,1},{18,2},{19,3},{20,4},{21,5},{22,6},{23,7},{24,8},{25... | collective-permute-start | bytes 98312 | tf_op jit(solution)/shard_map/ppermute | solution.py:37
  184.6 1.4 collective-permute-start.8
  186.0 1.3 collective-permute-start.7
  187.3 0.0 collective-permute-done.12
  187.3 0.0 collective-permute-done.11
  187.3 0.1 select_maximum_fusion
  187.4 0.1 fusion.80
  187.7 1.1 fusion.2
  188.8 0.0 collective-permute-done.8
  188.8 1.7 collective-permute-done.7
  190.5 4.5 %fusion.48 = f32[256,1,8,128]{3,2,1,0:T(8,128)} fusion(f32[256,1,8,128]{3,2,0,1:T(8,128)S(1)} %fusion.12, f32[256,8,128]{2,1,0:T(8,128)S(1)} %get-tuple-element.6, f32[256,8,128]{2,1,0:T(8,128)S(1)} %get-tuple-element.5, f32[256,1,8,128]{3,2,0,1:T(8,128)S(1)} %collective-permute-done.7, f32[256,1,8,128]{3,2,0,1:T(8,128)S(1)} %collective-permute-done.8, ...), kind=kLoop, calls=%fused_computation.82 | loop fusion | flops 9699328 | bytes 6341376 | tf_op jit(solution)/shard_map/jit(_where)/select_n | solution.py:142
  (28 shorter events, 0.4 us)
Async XLA Ops:
  1.8 82.9 %copy-start = (f32[256,1,8,128]{3,2,1,0:T(8,128)S(1)}, f32[256,1,8,128]{3,2,1,0:T(8,128)}, u32[]{:S(2)}) copy-start(f32[256,1,8,128]{3,2,1,0:T(8,128)} %param.3) | copy-start | bytes 3145732
  1.9 87.3 %copy-start.1 = (s32[3,1,8,128]{3,2,1,0:T(8,128)S(1)}, s32[3,1,8,128]{3,2,1,0:T(8,128)}, u32[]{:S(2)}) copy-start(s32[3,1,8,128]{3,2,1,0:T(8,128)} %param.4) | copy-start | bytes 36868
  1.9 88.7 %copy-start.2 = (s32[1,8,128]{2,1,0:T(8,128)S(1)}, s32[1,8,128]{2,1,0:T(8,128)}, u32[]{:S(2)}) copy-start(s32[1,8,128]{2,1,0:T(8,128)} %param.5) | copy-start | bytes 12292
  66.6 25.7 %collective-permute-start.4 = (f32[8,1,8,128]{3,0,2,1:T(8,128)S(1)}, f32[8,1,8,128]{3,0,2,1:T(8,128)S(1)}, u32[]{:S(2)}, u32[]{:S(2)}) collective-permute-start(f32[8,1,8,128]{3,0,2,1:T(8,128)S(1)} %psum.14), channel_id=1, source_target_pairs={{0,16},{1,17},{2,18},{3,19},{4,20},{5,21},{6,22},{7,23},{8,24},{9,... | collective-permute-start | bytes 98312 | tf_op jit(solution)/shard_map/ppermute | solution.py:35
  67.9 24.5 %collective-permute-start.3 = (f32[8,1,8,128]{3,0,2,1:T(8,128)S(1)}, f32[8,1,8,128]{3,0,2,1:T(8,128)S(1)}, u32[]{:S(2)}, u32[]{:S(2)}) collective-permute-start(f32[8,1,8,128]{3,0,2,1:T(8,128)S(1)} %psum.14), channel_id=1, source_target_pairs={{16,0},{17,1},{18,2},{19,3},{20,4},{21,5},{22,6},{23,7},{24,8},{25... | collective-permute-start | bytes 98312 | tf_op jit(solution)/shard_map/ppermute | solution.py:37
  84.7 14.5 %collective-permute-start.1 = (f32[256,1,8,128]{3,2,0,1:T(8,128)S(1)}, f32[256,1,8,128]{3,2,0,1:T(8,128)S(1)}, u32[]{:S(2)}, u32[]{:S(2)}) collective-permute-start(f32[256,1,8,128]{3,2,0,1:T(8,128)S(1)} %bitcast.157), channel_id=1, source_target_pairs={{0,16},{1,17},{2,18},{3,19},{4,20},{5,21},{6,22},{7,23},{8,24},{9,... | collective-permute-start | bytes 3145736 | tf_op jit(solution)/shard_map/ppermute | solution.py:35
  86.0 13.2 %collective-permute-start.2 = (f32[256,1,8,128]{3,2,0,1:T(8,128)S(1)}, f32[256,1,8,128]{3,2,0,1:T(8,128)S(1)}, u32[]{:S(2)}, u32[]{:S(2)}) collective-permute-start(f32[256,1,8,128]{3,2,0,1:T(8,128)S(1)} %bitcast.158), channel_id=1, source_target_pairs={{16,0},{17,1},{18,2},{19,3},{20,4},{21,5},{22,6},{23,7},{24,8},{25... | collective-permute-start | bytes 3145736 | tf_op jit(solution)/shard_map/ppermute | solution.py:37
  89.2 3.1 %collective-permute-start = (s32[1,8,128]{2,1,0:T(8,128)S(1)}, s32[1,8,128]{2,1,0:T(8,128)S(1)}, u32[]{:S(2)}, u32[]{:S(2)}) collective-permute-start(s32[1,8,128]{2,1,0:T(8,128)S(1)} %slice_bitcast_fusion.1), channel_id=1, source_target_pairs={{0,16},{1,17},{2,18},{3,19},{4,20},{5,21},{6,22},{7,23},{8,24},{9,... | collective-permute-start | bytes 12296 | tf_op jit(solution)/shard_map/ppermute | solution.py:24
  92.6 4.4 %collective-permute-start.6 = (f32[8,1,8,128]{3,0,2,1:T(8,128)S(1)}, f32[8,1,8,128]{3,0,2,1:T(8,128)S(1)}, u32[]{:S(2)}, u32[]{:S(2)}) collective-permute-start(f32[8,1,8,128]{3,0,2,1:T(8,128)S(1)} %fusion.56), channel_id=1, source_target_pairs={{0,16},{1,17},{2,18},{3,19},{4,20},{5,21},{6,22},{7,23},{8,24},{9,... | collective-permute-start | bytes 98312 | tf_op jit(solution)/shard_map/ppermute | solution.py:35
  93.9 3.9 %collective-permute-start.5 = (f32[8,1,8,128]{3,0,2,1:T(8,128)S(1)}, f32[8,1,8,128]{3,0,2,1:T(8,128)S(1)}, u32[]{:S(2)}, u32[]{:S(2)}) collective-permute-start(f32[8,1,8,128]{3,0,2,1:T(8,128)S(1)} %fusion.56), channel_id=1, source_target_pairs={{16,0},{17,1},{18,2},{19,3},{20,4},{21,5},{22,6},{23,7},{24,8},{25... | collective-permute-start | bytes 98312 | tf_op jit(solution)/shard_map/ppermute | solution.py:37
  161.8 17.5 %collective-permute-start.10 = (f32[8,1,8,128]{3,0,2,1:T(8,128)S(1)}, f32[8,1,8,128]{3,0,2,1:T(8,128)S(1)}, u32[]{:S(2)}, u32[]{:S(2)}) collective-permute-start(f32[8,1,8,128]{3,0,2,1:T(8,128)S(1)} %psum.15), channel_id=1, source_target_pairs={{0,16},{1,17},{2,18},{3,19},{4,20},{5,21},{6,22},{7,23},{8,24},{9,... | collective-permute-start | bytes 98312 | tf_op jit(solution)/shard_map/ppermute | solution.py:35
  163.1 17.0 %collective-permute-start.9 = (f32[8,1,8,128]{3,0,2,1:T(8,128)S(1)}, f32[8,1,8,128]{3,0,2,1:T(8,128)S(1)}, u32[]{:S(2)}, u32[]{:S(2)}) collective-permute-start(f32[8,1,8,128]{3,0,2,1:T(8,128)S(1)} %psum.15), channel_id=1, source_target_pairs={{16,0},{17,1},{18,2},{19,3},{20,4},{21,5},{22,6},{23,7},{24,8},{25... | collective-permute-start | bytes 98312 | tf_op jit(solution)/shard_map/ppermute | solution.py:37
  180.3 7.0 %collective-permute-start.12 = (f32[8,1,8,128]{3,0,2,1:T(8,128)S(1)}, f32[8,1,8,128]{3,0,2,1:T(8,128)S(1)}, u32[]{:S(2)}, u32[]{:S(2)}) collective-permute-start(f32[8,1,8,128]{3,0,2,1:T(8,128)S(1)} %fusion.72), channel_id=1, source_target_pairs={{0,16},{1,17},{2,18},{3,19},{4,20},{5,21},{6,22},{7,23},{8,24},{9,... | collective-permute-start | bytes 98312 | tf_op jit(solution)/shard_map/ppermute | solution.py:35
  181.6 5.7 %collective-permute-start.11 = (f32[8,1,8,128]{3,0,2,1:T(8,128)S(1)}, f32[8,1,8,128]{3,0,2,1:T(8,128)S(1)}, u32[]{:S(2)}, u32[]{:S(2)}) collective-permute-start(f32[8,1,8,128]{3,0,2,1:T(8,128)S(1)} %fusion.72), channel_id=1, source_target_pairs={{16,0},{17,1},{18,2},{19,3},{20,4},{21,5},{22,6},{23,7},{24,8},{25... | collective-permute-start | bytes 98312 | tf_op jit(solution)/shard_map/ppermute | solution.py:37
  184.6 4.2 %collective-permute-start.8 = (f32[256,1,8,128]{3,2,0,1:T(8,128)S(1)}, f32[256,1,8,128]{3,2,0,1:T(8,128)S(1)}, u32[]{:S(2)}, u32[]{:S(2)}) collective-permute-start(f32[256,1,8,128]{3,2,0,1:T(8,128)S(1)} %fusion.12), channel_id=1, source_target_pairs={{16,0},{17,1},{18,2},{19,3},{20,4},{21,5},{22,6},{23,7},{24,8},{25... | collective-permute-start | bytes 3145736 | tf_op jit(solution)/shard_map/ppermute | solution.py:37
  186.0 4.6 %collective-permute-start.7 = (f32[256,1,8,128]{3,2,0,1:T(8,128)S(1)}, f32[256,1,8,128]{3,2,0,1:T(8,128)S(1)}, u32[]{:S(2)}, u32[]{:S(2)}) collective-permute-start(f32[256,1,8,128]{3,2,0,1:T(8,128)S(1)} %fusion.12), channel_id=1, source_target_pairs={{0,16},{1,17},{2,18},{3,19},{4,20},{5,21},{6,22},{7,23},{8,24},{9,... | collective-permute-start | bytes 3145736 | tf_op jit(solution)/shard_map/ppermute | solution.py:35
where the time goes:
time: 196 us; the launch traced here: 195 us
  blocking collectives  122 us (62%)
  starting transfers between devices  52.6 us (27%)
  other arithmetic  11.1 us (6%)
  waiting for transfers between devices  5 us (3%)
  local copies, waits for them, and re-layouts  2.43 us (1%)
    psum x2, blocking collectives, body(): moments = lax.psum(partial_value, 'vel')  122 us
    ppermute x6, starting transfers between devices, padded_2(): lax.ppermute(head, axis, [((i + 1) % count, i) for i in range(ends)])  43.5 us
    ppermute x6, starting transfers between devices, padded_2(): lax.ppermute(tail, axis, [(i, (i + 1) % count) for i in range(ends)])  7.73 us
    select_n x2, other arithmetic, transport(): return jnp.where(solid > 0, dist, fresh)  7.63 us
  transfers between devices with their start and end apart: 13, of which 4 were waited for; matrix products, arithmetic and copies ran while one was open for 2% of the time, Pallas kernels for 0%

commit v1 on v0

v1 whole, which is shorter than its diff:
```python
import functools
import math

import jax
import jax.numpy as jnp
from jax import lax
from jax.experimental import pallas as pl
from jax.experimental.pallas import tpu as pltpu
from jax.sharding import PartitionSpec as P

NQ = 16
HALF = NQ // 2
SWEEPS = 2
MOMENTS = 8

SPACING = 0.6
COUPLING = 1.0
COURANT = 0.06
RELAXATION_FREQ = 0.5
VISCOUS_TO_HEAT = 2.0 / 3.0
QUAD_WEIGHT = SPACING**3 / (2.0 * math.pi) ** 1.5

MESH = pl.DeviceIdType.MESH


def speed_of(index):
    return (index.astype(jnp.float32) - (NQ - 1) / 2.0) * SPACING


def rolled(cells, shift, axis):
    size = cells.shape[axis]
    return pltpu.roll(cells, shift % size if isinstance(shift, int) else shift, axis)


def upper(cells):
    return jnp.concatenate([cells[1:], jnp.zeros_like(cells[:1])], axis=0)


def lower(cells):
    return jnp.concatenate([jnp.zeros_like(cells[:1]), cells[:-1]], axis=0)


def macro_state(predicted):
    rho = predicted[0]
    per_rho = 1.0 / rho
    u = [predicted[1 + a] * per_rho for a in range(3)]
    energy = predicted[4]
    temp = (2.0 * energy * per_rho - (u[0] * u[0] + u[1] * u[1] + u[2] * u[2])) / 3.0
    pressure = rho * temp
    nu = RELAXATION_FREQ * rho * jnp.exp(0.28 * jnp.log(temp))
    scale = (1.0 - VISCOUS_TO_HEAT) / (5.0 * pressure * temp)
    s = [(predicted[5 + a] - u[a] * (energy + pressure)) * scale for a in range(3)]
    root = lax.rsqrt(temp)
    return u, temp, nu, s, rho * (root * root * root)


def masked_state(predicted, solid):
    u, temp, nu, s, height = macro_state(predicted)
    fluid = solid == 0
    per_temp = jnp.where(fluid, 1.0 / temp, 1.0)
    u = [jnp.where(fluid, x, 0.0) for x in u]
    s = [jnp.where(fluid, x, 0.0) for x in s]
    inv = jnp.where(fluid, 1.0 / (1.0 + nu), 1.0)
    amp = jnp.where(fluid, height * (nu / (1.0 + nu)), 0.0)
    return u, per_temp, s, inv, amp


def goal_moments(u, per_temp, s, amp):
    def one(i, sums):
        xi = speed_of(i)
        new = []
        for a in range(3):
            c = xi - u[a]
            term = jnp.exp(-0.5 * (c * c * per_temp))
            row = [sums[a][0] + term]
            for k in range(1, 7):
                term = term * c
                row.append(sums[a][k] + term)
            new.append(tuple(row))
        return tuple(new)

    zero = jnp.zeros_like(per_temp)
    line = lax.fori_loop(0, NQ, one, tuple((zero,) * 7 for _ in range(3)), unroll=2)
    pairs, products, heats, lifts = {}, {}, {}, {}

    def add(m, a, n=1):
        return tuple(k + n * (a == d) for d, k in enumerate(m))

    def f(m):
        if m not in products:
            if m[:2] not in pairs:
                pairs[m[:2]] = line[0][m[0]] * line[1][m[1]]
            products[m] = pairs[m[:2]] * line[2][m[2]]
        return products[m]

    def q(m):
        if m not in heats:
            heats[m] = f(add(m, 0, 2)) + f(add(m, 1, 2)) + f(add(m, 2, 2))
        return heats[m]

    def lift(m):
        if m not in lifts:
            lifts[m] = per_temp * q(m) - 5.0 * f(m)
        return lifts[m]

    def total(m):
        out = f(m)
        for a in range(3):
            out = out + s[a] * lift(add(m, a))
        return out

    def total_q(m):
        out = q(m)
        for a in range(3):
            up = add(m, a)
            out = out + s[a] * (lift(add(up, 0, 2)) + lift(add(up, 1, 2)) + lift(add(up, 2, 2)))
        return out

    origin = (0, 0, 0)
    weight = amp * QUAD_WEIGHT
    p0 = total(origin) * weight
    p1 = [total(add(origin, a)) * weight for a in range(3)]
    p2 = {}
    for a in range(3):
        for b in range(a, 3):
            p2[a, b] = p2[b, a] = total(add(add(origin, a), b)) * weight
    p3 = [total_q(add(origin, a)) * weight for a in range(3)]
    half_uu = 0.5 * (u[0] * u[0] + u[1] * u[1] + u[2] * u[2])
    energy = (
        0.5 * (p2[0, 0] + p2[1, 1] + p2[2, 2])
        + (u[0] * p1[0] + u[1] * p1[1] + u[2] * p1[2])
        + half_uu * p0
    )
    out = [p0] + [p1[a] + u[a] * p0 for a in range(3)] + [energy]
    for a in range(3):
        out.append(
            0.5 * p3[a]
            + (u[0] * p2[a, 0] + u[1] * p2[a, 1] + u[2] * p2[a, 2])
            + half_uu * p1[a]
            + u[a] * energy
        )
    return out


def kernel(
    n_slab, n_vel, f_ref, links_ref, solid_ref, out_ref,
    f0, base, last, halo0, halo1, links_all, solid_all, send1, send2, gather_in, all1, all2,
    faces, coef, gx, pred,
    load_sem, link_sem, link_send, halo_recv, halo_send, rs_recv, rs_send, ag_recv, ag_send, out_sem,
):
    slab = lax.axis_index("slab")
    rank = lax.axis_index("vel")
    rows = f_ref.shape[0]
    first1 = n_vel // 2 - MOMENTS // 2
    first2 = n_vel // 2 + MOMENTS // 2
    plane1 = rank - first1
    plane2 = lax.rem(rank - first2 + n_vel, n_vel)
    reduces1 = (plane1 >= 0) & (plane1 < MOMENTS)
    reduces2 = plane2 < MOMENTS
    has_below = slab > 0
    has_above = slab < n_slab - 1

    def start_all(copies):
        for copy in copies:
            copy.start()

    loads = [
        pltpu.make_async_copy(f_ref, f0, load_sem.at[0]),
        pltpu.make_async_copy(links_ref, links_all.at[slab], load_sem.at[1]),
        pltpu.make_async_copy(solid_ref, solid_all.at[slab], load_sem.at[2]),
    ]
    start_all(loads)

    barrier = pltpu.get_barrier_semaphore()
    for step in range(n_slab):
        to_slab = lax.rem(slab + step, n_slab)

        def greet(i, _, to_slab=to_slab):
            pl.semaphore_signal(
                barrier, inc=1, device_id={"slab": to_slab, "vel": lax.rem(rank + i, n_vel)},
                device_id_type=MESH,
            )
            return 0

        lax.fori_loop(1 if step == 0 else 0, n_vel, greet, 0)

    def clear(low):
        def one(j, _):
            for i in range(HALF):
                zero = jnp.zeros(f0.shape[2:], jnp.float32)
                halo0[j, low + i] = zero
                halo1[j, low + i] = zero
            return 0

        lax.fori_loop(0, rows, one, 0)

    @pl.when(jnp.logical_not(has_below))
    def _():
        clear(HALF)

    @pl.when(jnp.logical_not(has_above))
    def _():
        clear(0)

    def row_speeds(j):
        row = rank * rows + j
        return lax.rem(row, NQ), lax.div(row, NQ)

    def add_row(sums, a0, a1, a2, a3, xi_y, xi_z):
        r = xi_y * xi_y + xi_z * xi_z
        e = 0.5 * (a2 + r * a0)
        return (
            sums[0] + a0, sums[1] + a1, sums[2] + xi_y * a0, sums[3] + xi_z * a0,
            sums[4] + e, sums[5] + 0.5 * (a3 + r * a1), sums[6] + xi_y * e, sums[7] + xi_z * e,
        )

    def moments_of(source):
        def one(j, sums):
            y, z = row_speeds(j)
            a0 = a1 = a2 = a3 = None
            for i in range(HALF):
                xi = (i + 0.5) * SPACING
                plus, minus = source[j, HALF + i], source[j, HALF - 1 - i]
                even, odd = plus + minus, plus - minus
                t = [even * QUAD_WEIGHT, odd * (QUAD_WEIGHT * xi),
                     even * (QUAD_WEIGHT * xi**2), odd * (QUAD_WEIGHT * xi**3)]
                if i == 0:
                    a0, a1, a2, a3 = t
                else:
                    a0, a1, a2, a3 = a0 + t[0], a1 + t[1], a2 + t[2], a3 + t[3]
            return add_row(sums, a0, a1, a2, a3, speed_of(y), speed_of(z))

        zero = jnp.zeros(f0.shape[2:], jnp.float32)
        return lax.fori_loop(0, rows, one, (zero,) * MOMENTS)

    loads[0].wait()
    m1 = moments_of(f0)
    for k in range(MOMENTS):
        send1[k] = m1[k]
    loads[1].wait()
    loads[2].wait()
    pl.semaphore_wait(barrier, n_slab * n_vel - 1)

    def scatter(source, first):
        def one(i, _):
            k = lax.rem(rank + i, MOMENTS)
            target = lax.rem(first + k, n_vel)

            @pl.when(target != rank)
            def _():
                pltpu.make_async_remote_copy(
                    src_ref=source.at[k], dst_ref=gather_in.at[rank],
                    send_sem=rs_send.at[0 if source is send1 else 1], recv_sem=rs_recv,
                    device_id={"vel": target}, device_id_type=MESH,
                ).start()

            return 0

        lax.fori_loop(0, MOMENTS, one, 0)

    scatter(send1, first1)

    for step in range(1, n_slab):
        to_slab = lax.rem(slab + step, n_slab)
        pltpu.make_async_remote_copy(
            src_ref=links_ref, dst_ref=links_all.at[slab], send_sem=link_send.at[0, step],
            recv_sem=link_sem.at[0], device_id={"slab": to_slab}, device_id_type=MESH,
        ).start()
        pltpu.make_async_remote_copy(
            src_ref=solid_ref, dst_ref=solid_all.at[slab], send_sem=link_send.at[1, step],
            recv_sem=link_sem.at[1], device_id={"slab": to_slab}, device_id_type=MESH,
        ).start()

    up_half, low_half = pl.ds(HALF, HALF), pl.ds(0, HALF)

    def halo_copy(source, halo, which, half):
        part = up_half if half else low_half
        to_slab = slab + 1 if half else slab - 1
        return pltpu.make_async_remote_copy(
            src_ref=source.at[:, part], dst_ref=halo.at[:, part],
            send_sem=halo_send.at[which, half], recv_sem=halo_recv.at[which, half],
            device_id={"slab": to_slab}, device_id_type=MESH,
        )

    def send_halo(source, halo, which):
        @pl.when(has_above)
        def _():
            halo_copy(source, halo, which, 1).start()

        @pl.when(has_below)
        def _():
            halo_copy(source, halo, which, 0).start()

    def wait_halo(source, halo, which, half):
        @pl.when(has_below if half else has_above)
        def _():
            halo_copy(source, halo, which, half).wait_recv()

    def wait_halo_send(source, halo, which):
        @pl.when(has_above)
        def _():
            halo_copy(source, halo, which, 1).wait_send()

        @pl.when(has_below)
        def _():
            halo_copy(source, halo, which, 0).wait_send()

    send_halo(f0, halo0, 0)

    if n_slab > 1:
        others = pl.ds(0, n_slab - 1)
        pltpu.make_async_copy(links_all.at[others], links_all.at[others], link_sem.at[0]).wait()
        pltpu.make_async_copy(solid_all.at[others], solid_all.at[others], link_sem.at[1]).wait()

    shape = (n_slab,) + f0.shape[2:]
    up = [links_all[:, a].astype(jnp.float32) for a in range(3)]
    at_y = lax.broadcasted_iota(jnp.int32, shape, 1)
    at_z = lax.broadcasted_iota(jnp.int32, shape, 2)
    at_x = lax.broadcasted_iota(jnp.int32, shape, 0)
    low = [
        lower(up[0]),
        jnp.where(at_y == 0, 0.0, rolled(up[1], 1, 1)),
        jnp.where(at_z == 0, 0.0, rolled(up[2], 1, 2)),
    ]
    up_in = [
        jnp.where(at_x == shape[0] - 1, 0.0, up[0]),
        jnp.where(at_y == shape[1] - 1, 0.0, up[1]),
        jnp.where(at_z == shape[2] - 1, 0.0, up[2]),
    ]
    count = up[0] + up[1] + up[2] + low[0] + low[1] + low[2]
    for a in range(3):
        faces[a] = up_in[a]
        faces[3 + a] = low[a]
    faces[6] = 1.0 / (1.0 + COUPLING * count)
    solid = solid_all[...]
    fluid = jnp.where(solid == 0, COURANT, 0.0)
    for a in range(3):
        pred[0] = fluid * low[a]
        pred[1] = fluid * up_in[a]
        pred[2] = fluid * up[a]
        coef[0, a, 0] = pred[0, slab]
        coef[0, a, 1] = pred[1, slab]
        coef[1, a, 0] = pred[2, slab]
        coef[1, a, 1] = pred[0, slab]

    def streamed(source, halo, half, first_row, row_end, finish):
        cells = f0.shape[2:]

        def one(j, carry):
            y, z = row_speeds(j)
            xi_y, xi_z = speed_of(y), speed_of(z)
            sign_y = jnp.where(y >= HALF, 1, 0)
            sign_z = jnp.where(z >= HALF, 1, 0)
            turn_y = jnp.where(y >= HALF, 1, cells[0] - 1)
            turn_z = jnp.where(z >= HALF, 1, cells[1] - 1)
            abs_y, abs_z = jnp.abs(xi_y), jnp.abs(xi_z)
            stay = 1.0 - (abs_y * coef[sign_y, 1, 0] + abs_z * coef[sign_z, 2, 0])
            in_y = abs_y * coef[sign_y, 1, 1]
            in_z = abs_z * coef[sign_z, 2, 1]
            out_x, in_x = coef[half, 0, 0], coef[half, 0, 1]
            extra = finish.row(j, xi_y, xi_z) if finish else None
            for i in range(HALF):
                ix = half * HALF + i
                abs_x = jnp.abs(speed_of(jnp.int32(ix))) if isinstance(ix, int) else jnp.abs(speed_of(ix))
                f = source[j, ix]
                value = (
                    f * (stay - abs_x * out_x)
                    + in_y * rolled(f, turn_y, 0)
                    + in_z * rolled(f, turn_z, 1)
                    + abs_x * (in_x * halo[j, ix])
                )
                if finish:
                    finish.store(j, ix, value, extra)
                else:
                    base[j, ix] = value
            return carry

        lax.fori_loop(first_row, row_end, one, 0)

    class Goal:
        def __init__(self, target, u, per_temp, s, inv, amp):
            self.target, self.u, self.per_temp, self.s, self.inv, self.amp = target, u, per_temp, s, inv, amp

            def one(i, _):
                c = speed_of(i) - u[0]
                part = c * c * per_temp
                gx[0, i] = jnp.exp(-0.5 * part)
                gx[1, i] = s[0] * c
                gx[2, i] = part
                return 0

            lax.fori_loop(0, NQ, one, 0, unroll=4)

        def row(self, j, xi_y, xi_z):
            c_y, c_z = xi_y - self.u[1], xi_z - self.u[2]
            part = (c_y * c_y + c_z * c_z) * self.per_temp
            return jnp.exp(-0.5 * part) * self.amp, self.s[1] * c_y + self.s[2] * c_z, part - 5.0

        def store(self, j, ix, value, extra):
            height, along, part = extra
            bell = gx[0, ix] * height
            self.target[j, ix] = value * self.inv + bell * (1.0 + (gx[1, ix] + along) * (gx[2, ix] + part))

    lead = jnp.where(has_above, 1, 0)

    def both_halves(body):
        for turn in range(2):
            body(lead if turn == 0 else 1 - lead, turn)

    def wait_dynamic(source, halo, which, half):
        @pl.when(half == 1)
        def _():
            wait_halo(source, halo, which, 1)

        @pl.when(half == 0)
        def _():
            wait_halo(source, halo, which, 0)

    def reduce_and_send(plane, source, everything, which):
        pltpu.make_async_copy(
            gather_in.at[pl.ds(0, n_vel - 1)], gather_in.at[pl.ds(0, n_vel - 1)], rs_recv
        ).wait()
        gather_in[rank] = source[plane]
        total = gather_in[0]
        for v in range(1, n_vel):
            total = total + gather_in[v]
        mine = plane * n_slab + slab
        everything[mine] = total
        for step in range(n_slab):
            to_slab = lax.rem(slab + step, n_slab)

            def one(i, _, to_slab=to_slab, step=step):
                pltpu.make_async_remote_copy(
                    src_ref=everything.at[mine], dst_ref=everything.at[mine],
                    send_sem=ag_send.at[step], recv_sem=ag_recv.at[which],
                    device_id={"slab": to_slab, "vel": lax.rem(rank + i, n_vel)}, device_id_type=MESH,
                ).start()
                return 0

            lax.fori_loop(1 if step == 0 else 0, n_vel, one, 0)

    def wait_gathered(everything, which, reduces):
        planes = MOMENTS * n_slab

        @pl.when(reduces)
        def _():
            part = everything.at[pl.ds(0, planes - 1)]
            pltpu.make_async_copy(part, part, ag_recv.at[which]).wait()

        @pl.when(jnp.logical_not(reduces))
        def _():
            pltpu.make_async_copy(everything, everything, ag_recv.at[which]).wait()

    def first_pass(half, turn):
        wait_dynamic(f0, halo0, 0, half)
        streamed(f0, halo0, half, 0, rows, None)

    first_pass(lead, 0)

    @pl.when(reduces1)
    def _():
        reduce_and_send(plane1, send1, all1, 0)

    first_pass(1 - lead, 1)
    m2 = moments_of(base)
    for k in range(MOMENTS):
        send2[k] = m2[k]
    scatter(send2, first2)

    def predict(moments):
        now = moments
        for _ in range(SWEEPS):
            beside = (
                upper(now) * faces[0] + lower(now) * faces[3]
                + rolled(now, -1, 1) * faces[1] + rolled(now, 1, 1) * faces[4]
                + rolled(now, -1, 2) * faces[2] + rolled(now, 1, 2) * faces[5]
            )
            now = (moments + COUPLING * beside) * faces[6]
        return now

    wait_gathered(all1, 0, reduces1)
    state1 = [predict(all1[k * n_slab:(k + 1) * n_slab]) for k in range(MOMENTS)]
    u, per_temp, s, inv, amp = masked_state(state1, solid)

    def own(planes):
        for k, plane in enumerate(planes):
            pred[k] = plane
        return [pred[k, slab] for k in range(len(planes))]

    near = own([*u, per_temp, *s, inv])
    near_amp = own([amp])[0]
    goal = Goal(base, near[0:3], near[3], near[4:7], near[7], near_amp)

    def relax_rows(half):
        def one(j, carry):
            y, z = row_speeds(j)
            extra = goal.row(j, speed_of(y), speed_of(z))
            for i in range(HALF):
                goal.store(j, half * HALF + i, base[j, half * HALF + i], extra)
            return carry

        lax.fori_loop(0, rows, one, 0)

    relax_rows(lead)

    @pl.when(lead == 1)
    def _():
        @pl.when(has_above)
        def _():
            halo_copy(base, halo1, 1, 1).start()

    @pl.when(lead == 0)
    def _():
        @pl.when(has_below)
        def _():
            halo_copy(base, halo1, 1, 0).start()

    @pl.when(reduces2)
    def _():
        reduce_and_send(plane2, send2, all2, 1)

    relax_rows(1 - lead)

    @pl.when(jnp.logical_and(lead == 1, has_below))
    def _():
        halo_copy(base, halo1, 1, 0).start()

    target = goal_moments(u, per_temp, s, amp)

    wait_gathered(all2, 1, reduces2)
    state2 = [
        predict(all2[k * n_slab:(k + 1) * n_slab] * inv + target[k]) for k in range(MOMENTS)
    ]
    u, per_temp, s, inv, amp = masked_state(state2, solid)
    near = own([*u, per_temp, *s, inv])
    near_amp = own([amp])[0]
    final = Goal(last, near[0:3], near[3], near[4:7], near[7], near_amp)

    stores = []

    def last_pass(half, turn):
        wait_dynamic(base, halo1, 1, half)
        cut = rows // 2
        for piece in range(2):
            streamed(base, halo1, half, piece * cut, (piece + 1) * cut, final)
            where = (pl.ds(piece * cut, cut), pl.ds(half * HALF, HALF))
            copy = pltpu.make_async_copy(last.at[where], out_ref.at[where], out_sem.at[turn, piece])
            copy.start()
            stores.append(copy)

    both_halves(last_pass)

    wait_halo_send(f0, halo0, 0)
    wait_halo_send(base, halo1, 1)
    for step in range(1, n_slab):
        pltpu.make_async_copy(links_all.at[0], links_all.at[0], link_send.at[0, step]).wait()
        pltpu.make_async_copy(solid_all.at[0], solid_all.at[0], link_send.at[1, step]).wait()
    for which, reduces in ((0, reduces1), (1, reduces2)):
        source = send1 if which == 0 else send2

        @pl.when(reduces)
        def _():
            part = source.at[pl.ds(0, MOMENTS - 1)]
            pltpu.make_async_copy(part, part, rs_send.at[which]).wait()
            for step in range(n_slab):
                part = gather_in.at[pl.ds(0, n_vel - 1 if step == 0 else n_vel)]
                pltpu.make_async_copy(part, part, ag_send.at[step]).wait()

        @pl.when(jnp.logical_not(reduces))
        def _():
            pltpu.make_async_copy(source, source, rs_send.at[which]).wait()

    for copy in stores:
        copy.wait()


def body(f_start, links, solid):
    n_slab, n_vel = lax.axis_size("slab"), lax.axis_size("vel")
    vel_local, planes = f_start.shape[:2]
    cells = f_start.shape[2:]
    rows = vel_local // NQ
    assert planes == 1 and rows * NQ == vel_local and rows % 2 == 0 and n_vel >= 2 * MOMENTS
    f32, vmem, dma = jnp.float32, pltpu.VMEM, pltpu.SemaphoreType.DMA
    block = (rows, NQ) + cells
    grid = (n_slab,) + cells
    any_spec = pl.BlockSpec(memory_space=pl.ANY)
    out = pl.pallas_call(
        functools.partial(kernel, n_slab, n_vel),
        out_shape=jax.ShapeDtypeStruct(block, f32),
        in_specs=[any_spec] * 3,
        out_specs=any_spec,
        scratch_shapes=[
            vmem(block, f32), vmem(block, f32), vmem(block, f32), vmem(block, f32), vmem(block, f32),
            vmem((n_slab, 3) + cells, jnp.int32), vmem(grid, jnp.int32),
            vmem((MOMENTS,) + cells, f32), vmem((MOMENTS,) + cells, f32),
            vmem((n_vel,) + cells, f32),
            vmem((MOMENTS * n_slab,) + cells, f32), vmem((MOMENTS * n_slab,) + cells, f32),
            vmem((7,) + grid, f32), vmem((2, 3, 2) + cells, f32), vmem((3, NQ) + cells, f32),
            vmem((MOMENTS,) + grid, f32),
            dma((3,)), dma((2,)), dma((2, n_slab)), dma((2, 2)), dma((2, 2)), dma, dma((2,)),
            dma((2,)), dma((n_slab,)), dma((2, 2)),
        ],
        compiler_params=pltpu.CompilerParams(
            collective_id=0, has_side_effects=True, vmem_limit_bytes=32 * 1024 * 1024
        ),
    )(f_start.reshape(block), links.reshape((3,) + cells), solid.reshape(cells))
    return out.reshape(f_start.shape)


def solution(mesh):
    in_specs = (P("vel", "slab", None, None), P(None, "slab", None, None), P("slab", None, None))
    out_specs = P("vel", "slab", None, None)
    return jax.shard_map(body, mesh=mesh, in_specs=in_specs, out_specs=out_specs, check_vma=False)
```

time: 196 us -> 27.8 us (0.14)
  blocking collectives: 122 us -> 0 us
  starting transfers between devices: 52.6 us -> 0 us
  Pallas kernels: 0 us -> 23.9 us
  other arithmetic: 11.1 us -> 0 us
  waiting for transfers between devices: 5 us -> 0 us
    psum x2 -> x0, blocking collectives: 122 us -> none  [body(): moments = lax.psum(partial_value, 'vel')]
    ppermute x13 -> x0, starting transfers between devices: 52.6 us -> none  [the longest x6 43.5 us: padded_2(): lax.ppermute(head, axis, [((i + 1) % count, i) for i in range(ends)])]
    pallas_call x0 -> x1, Pallas kernels: none -> 23.9 us  [body(): pl.pallas_call(functools.partial(kernel, n_slab, n_vel), out_shape=jax.Sh...]
    select_n x4 -> x0, other arithmetic: 7.67 us -> none  [the longest x2 7.63 us: transport(): return jnp.where(solid > 0, dist, fresh)]
    ppermute x13 -> x0, waiting for transfers between devices: 5 us -> none  [the longest x6 1.73 us: padded_2(): lax.ppermute(tail, axis, [(i, (i + 1) % count) for i in range(ends)])]
    reduce_sum x6 -> x0, other arithmetic: 2.3 us -> none  [the longest x2 2.22 us: transport(): acoustic_celerity_power = jnp.sum(peculiar * peculiar, axis=0)]
  transfers between devices with their start and end apart: 13 -> 0, of which waited for: 4 -> 0; matrix products, arithmetic and copies ran while one was open for 2% -> 0% of each run, Pallas kernels for 0% -> 0%
where the time goes in v1:
time: 27.8 us; the launch traced here: 27.6 us
  Pallas kernels  23.9 us (86%)
  local copies, waits for them, and re-layouts  3.59 us (13%)
    pallas_call x1, Pallas kernels, body(): pl.pallas_call(functools.partial(kernel, n_slab, n_vel), out_shape=jax.Sh...  23.9 us
    unnamed x7, local copies, waits for them, and re-layouts  3.59 us

profile of v1, /device:TPU:1, one launch (start us, length us, event | category | flops | bytes accessed | tf_op | source)
XLA Modules:
  0.0 27.6 jit_solution(15039251231067564764)
XLA Ops:
  0.0 0.0 copy-start.2
  0.0 0.7 %copy-done.2 = s32[1,8,128]{2,1,0:T(8,128)S(1)} copy-done((s32[1,8,128]{2,1,0:T(8,128)S(1)}, s32[1,8,128]{2,1,0:T(8,128)}, u32[]{:S(2)}) %copy-start.2) | copy-done | bytes 4120
  0.7 0.0 copy-start
  0.7 1.2 %copy-done = f32[256,1,8,128]{3,2,1,0:T(8,128)S(1)} copy-done((f32[256,1,8,128]{3,2,1,0:T(8,128)S(1)}, f32[256,1,8,128]{3,2,1,0:T(8,128)}, u32[]{:S(2)}) %copy-start) | copy-done | bytes 1048600
  1.9 0.0 copy-start.1
  1.9 0.7 %copy-done.1 = s32[3,1,8,128]{3,2,1,0:T(8,128)S(1)} copy-done((s32[3,1,8,128]{3,2,1,0:T(8,128)S(1)}, s32[3,1,8,128]{3,2,1,0:T(8,128)}, u32[]{:S(2)}) %copy-start.1) | copy-done | bytes 12312
  2.6 23.9 %shard_map.37 = f32[16,16,8,128]{3,2,1,0:T(8,128)S(1)} custom-call(f32[16,16,8,128]{3,2,1,0:T(8,128)S(1)} %bitcast.7, s32[3,8,128]{2,1,0:T(8,128)S(1)} %bitcast.8, s32[8,128]{1,0:T(8,128)S(1)} %bitcast.9), custom_call_target="tpu_custom_call" | custom-call | tf_op jit(solution)/shard_map/pallas_call | solution.py:587
  26.6 1.0 %copy.6 = f32[256,1,8,128]{3,2,1,0:T(8,128)} copy(f32[256,1,8,128]{3,2,1,0:T(8,128)S(1)} %bitcast.6) | data formatting | bytes 2097152
Async XLA Ops:
  0.0 0.7 %copy-start.2 = (s32[1,8,128]{2,1,0:T(8,128)S(1)}, s32[1,8,128]{2,1,0:T(8,128)}, u32[]{:S(2)}) copy-start(s32[1,8,128]{2,1,0:T(8,128)} %param.5) | copy-start | bytes 12292
  0.7 1.2 %copy-start = (f32[256,1,8,128]{3,2,1,0:T(8,128)S(1)}, f32[256,1,8,128]{3,2,1,0:T(8,128)}, u32[]{:S(2)}) copy-start(f32[256,1,8,128]{3,2,1,0:T(8,128)} %param.3) | copy-start | bytes 3145732
  1.9 0.7 %copy-start.1 = (s32[3,1,8,128]{3,2,1,0:T(8,128)S(1)}, s32[3,1,8,128]{3,2,1,0:T(8,128)}, u32[]{:S(2)}) copy-start(s32[3,1,8,128]{3,2,1,0:T(8,128)} %param.4) | copy-start | bytes 36868

commit v2 on v1

--- a/solution.py
+++ b/solution.py
@@ -80,7 +80,7 @@
         return tuple(new)
 
     zero = jnp.zeros_like(per_temp)
-    line = lax.fori_loop(0, NQ, one, tuple((zero,) * 7 for _ in range(3)), unroll=2)
+    line = lax.fori_loop(0, NQ, one, tuple((zero,) * 7 for _ in range(3)), unroll=4)
     pairs, products, heats, lifts = {}, {}, {}, {}
 
     def add(m, a, n=1):
@@ -182,7 +182,7 @@
             )
             return 0
 
-        lax.fori_loop(1 if step == 0 else 0, n_vel, greet, 0)
+        lax.fori_loop(1 if step == 0 else 0, n_vel, greet, 0, unroll=5 if step == 0 else 4)
 
     def clear(low):
         def one(j, _):
@@ -231,7 +231,7 @@
             return add_row(sums, a0, a1, a2, a3, speed_of(y), speed_of(z))
 
         zero = jnp.zeros(f0.shape[2:], jnp.float32)
-        return lax.fori_loop(0, rows, one, (zero,) * MOMENTS)
+        return lax.fori_loop(0, rows, one, (zero,) * MOMENTS, unroll=2)
 
     loads[0].wait()
     m1 = moments_of(f0)
@@ -256,7 +256,7 @@
 
             return 0
 
-        lax.fori_loop(0, MOMENTS, one, 0)
+        lax.fori_loop(0, MOMENTS, one, 0, unroll=True)
 
     scatter(send1, first1)
 
@@ -345,6 +345,7 @@
 
     def streamed(source, halo, half, first_row, row_end, finish):
         cells = f0.shape[2:]
+        abs_of = [jnp.abs(speed_of(half * HALF + i)) for i in range(HALF)]
 
         def one(j, carry):
             y, z = row_speeds(j)
@@ -361,7 +362,7 @@
             extra = finish.row(j, xi_y, xi_z) if finish else None
             for i in range(HALF):
                 ix = half * HALF + i
-                abs_x = jnp.abs(speed_of(jnp.int32(ix))) if isinstance(ix, int) else jnp.abs(speed_of(ix))
+                abs_x = abs_of[i]
                 f = source[j, ix]
                 value = (
                     f * (stay - abs_x * out_x)
@@ -375,7 +376,7 @@
                     base[j, ix] = value
             return carry
 
-        lax.fori_loop(first_row, row_end, one, 0)
+        lax.fori_loop(first_row, row_end, one, 0, unroll=math.gcd(4, row_end - first_row))
 
     class Goal:
         def __init__(self, target, u, per_temp, s, inv, amp):
@@ -437,7 +438,7 @@
                 ).start()
                 return 0
 
-            lax.fori_loop(1 if step == 0 else 0, n_vel, one, 0)
+            lax.fori_loop(1 if step == 0 else 0, n_vel, one, 0, unroll=5 if step == 0 else 4)
 
     def wait_gathered(everything, which, reduces):
         planes = MOMENTS * n_slab
@@ -499,7 +500,7 @@
                 goal.store(j, half * HALF + i, base[j, half * HALF + i], extra)
             return carry
 
-        lax.fori_loop(0, rows, one, 0)
+        lax.fori_loop(0, rows, one, 0, unroll=math.gcd(4, rows))
 
     relax_rows(lead)
 
@@ -583,7 +584,7 @@
     f32, vmem, dma = jnp.float32, pltpu.VMEM, pltpu.SemaphoreType.DMA
     block = (rows, NQ) + cells
     grid = (n_slab,) + cells
-    any_spec = pl.BlockSpec(memory_space=pl.ANY)
+    any_spec = pl.BlockSpec(memory_space=pltpu.HBM)
     out = pl.pallas_call(
         functools.partial(kernel, n_slab, n_vel),
         out_shape=jax.ShapeDtypeStruct(block, f32),

time: 27.8 us -> 25.7 us (0.924)
  Pallas kernels: 23.9 us -> 21.8 us
    pallas_call x1, Pallas kernels: 23.9 us -> 21.8 us  [body(): pl.pallas_call(functools.partial(kernel, n_slab, n_vel), out_shape=jax.Sh...]
where the time goes in v2:
time: 25.7 us; the launch traced here: 25.4 us
  Pallas kernels  21.8 us (85%)
  local copies, waits for them, and re-layouts  3.59 us (14%)
    pallas_call x1, Pallas kernels, body(): pl.pallas_call(functools.partial(kernel, n_slab, n_vel), out_shape=jax.Sh...  21.8 us
    unnamed x7, local copies, waits for them, and re-layouts  3.59 us

profile of v2, /device:TPU:1, one launch (start us, length us, event | category | flops | bytes accessed | tf_op | source)
XLA Modules:
  0.0 25.4 jit_solution(15240379473498924347)
XLA Ops:
  0.0 0.0 copy-start.2
  0.0 0.7 %copy-done.2 = s32[1,8,128]{2,1,0:T(8,128)S(1)} copy-done((s32[1,8,128]{2,1,0:T(8,128)S(1)}, s32[1,8,128]{2,1,0:T(8,128)}, u32[]{:S(2)}) %copy-start.2) | copy-done | bytes 4120
  0.7 0.0 copy-start
  0.7 1.2 %copy-done = f32[256,1,8,128]{3,2,1,0:T(8,128)S(1)} copy-done((f32[256,1,8,128]{3,2,1,0:T(8,128)S(1)}, f32[256,1,8,128]{3,2,1,0:T(8,128)}, u32[]{:S(2)}) %copy-start) | copy-done | bytes 1048600
  1.9 0.0 copy-start.1
  1.9 0.7 %copy-done.1 = s32[3,1,8,128]{3,2,1,0:T(8,128)S(1)} copy-done((s32[3,1,8,128]{3,2,1,0:T(8,128)S(1)}, s32[3,1,8,128]{3,2,1,0:T(8,128)}, u32[]{:S(2)}) %copy-start.1) | copy-done | bytes 12312
  2.6 21.8 %shard_map.37 = f32[16,16,8,128]{3,2,1,0:T(8,128)S(1)} custom-call(f32[16,16,8,128]{3,2,1,0:T(8,128)S(1)} %bitcast.7, s32[3,8,128]{2,1,0:T(8,128)S(1)} %bitcast.8, s32[8,128]{1,0:T(8,128)S(1)} %bitcast.9), custom_call_target="tpu_custom_call" | custom-call | tf_op jit(solution)/shard_map/pallas_call | solution.py:588
  24.4 1.0 %copy.6 = f32[256,1,8,128]{3,2,1,0:T(8,128)} copy(f32[256,1,8,128]{3,2,1,0:T(8,128)S(1)} %bitcast.6) | data formatting | bytes 2097152
Async XLA Ops:
  0.0 0.7 %copy-start.2 = (s32[1,8,128]{2,1,0:T(8,128)S(1)}, s32[1,8,128]{2,1,0:T(8,128)}, u32[]{:S(2)}) copy-start(s32[1,8,128]{2,1,0:T(8,128)} %param.5) | copy-start | bytes 12292
  0.7 1.2 %copy-start = (f32[256,1,8,128]{3,2,1,0:T(8,128)S(1)}, f32[256,1,8,128]{3,2,1,0:T(8,128)}, u32[]{:S(2)}) copy-start(f32[256,1,8,128]{3,2,1,0:T(8,128)} %param.3) | copy-start | bytes 3145732
  1.9 0.7 %copy-start.1 = (s32[3,1,8,128]{3,2,1,0:T(8,128)S(1)}, s32[3,1,8,128]{3,2,1,0:T(8,128)}, u32[]{:S(2)}) copy-start(s32[3,1,8,128]{3,2,1,0:T(8,128)} %param.4) | copy-start | bytes 36868

commit v3 on v2

--- a/solution.py
+++ b/solution.py
@@ -458,15 +458,15 @@
 
     first_pass(lead, 0)
 
-    @pl.when(reduces1)
-    def _():
-        reduce_and_send(plane1, send1, all1, 0)
-
     first_pass(1 - lead, 1)
     m2 = moments_of(base)
     for k in range(MOMENTS):
         send2[k] = m2[k]
     scatter(send2, first2)
+
+    @pl.when(reduces1)
+    def _():
+        reduce_and_send(plane1, send1, all1, 0)
 
     def predict(moments):
         now = moments
@@ -479,6 +479,10 @@
             now = (moments + COUPLING * beside) * faces[6]
         return now
 
+    @pl.when(reduces2)
+    def _():
+        reduce_and_send(plane2, send2, all2, 1)
+
     wait_gathered(all1, 0, reduces1)
     state1 = [predict(all1[k * n_slab:(k + 1) * n_slab]) for k in range(MOMENTS)]
     u, per_temp, s, inv, amp = masked_state(state1, solid)
@@ -515,10 +519,6 @@
         @pl.when(has_below)
         def _():
             halo_copy(base, halo1, 1, 0).start()
-
-    @pl.when(reduces2)
-    def _():
-        reduce_and_send(plane2, send2, all2, 1)
 
     relax_rows(1 - lead)
 
@@ -602,7 +602,7 @@
             dma((2,)), dma((n_slab,)), dma((2, 2)),
         ],
         compiler_params=pltpu.CompilerParams(
-            collective_id=0, has_side_effects=True, vmem_limit_bytes=32 * 1024 * 1024
+            collective_id=0, has_side_effects=True, vmem_limit_bytes=60 * 1024 * 1024
         ),
     )(f_start.reshape(block), links.reshape((3,) + cells), solid.reshape(cells))
     return out.reshape(f_start.shape)

time: 25.7 us -> 23.3 us (0.907)
  local copies, waits for them, and re-layouts: 3.59 us -> 2.26 us
  Pallas kernels: 21.8 us -> 20.8 us
    unnamed x7 -> x1, local copies, waits for them, and re-layouts: 3.59 us -> 2.26 us
    pallas_call x1, Pallas kernels: 21.8 us -> 20.8 us  [body(): pl.pallas_call(functools.partial(kernel, n_slab, n_vel), out_shape=jax.Sh...]
where the time goes in v3:
time: 23.3 us; the launch traced here: 23 us
  Pallas kernels  20.8 us (89%)
  local copies, waits for them, and re-layouts  2.26 us (10%)
    pallas_call x1, Pallas kernels, body(): pl.pallas_call(functools.partial(kernel, n_slab, n_vel), out_shape=jax.Sh...  20.8 us
    unnamed x1, local copies, waits for them, and re-layouts  2.26 us

profile of v3, /device:TPU:1, one launch (start us, length us, event | category | flops | bytes accessed | tf_op | source)
XLA Modules:
  0.0 23.0 jit_solution(8652335628361175861)
XLA Ops:
  0.0 20.8 %shard_map.37 = f32[16,16,8,128]{3,2,1,0:T(8,128)} custom-call(f32[16,16,8,128]{3,2,1,0:T(8,128)} %bitcast.7, s32[3,8,128]{2,1,0:T(8,128)} %bitcast.8, s32[8,128]{1,0:T(8,128)} %bitcast.9), custom_call_target="tpu_custom_call" | custom-call | tf_op jit(solution)/shard_map/pallas_call | solution.py:588
  20.8 2.3 %copy.6 = f32[256,1,8,128]{3,2,1,0:T(8,128)} copy(f32[256,1,8,128]{3,2,1,0:T(8,128)} %bitcast.6) | data formatting | bytes 2097152

commit v4 on v3

--- a/solution.py
+++ b/solution.py
@@ -142,11 +142,88 @@
     return out
 
 
+def upwind(source, halo, coef, half, speeds, size, store, row=None):
+    cells = source.shape[2:]
+    abs_of = [jnp.abs(speed_of(jnp.asarray(half * HALF + i))) for i in range(HALF)]
+
+    def one(j, carry):
+        y, z = speeds(j)
+        xi_y, xi_z = speed_of(y), speed_of(z)
+        sign_y = jnp.where(y >= HALF, 1, 0)
+        sign_z = jnp.where(z >= HALF, 1, 0)
+        turn_y = jnp.where(y >= HALF, 1, cells[0] - 1)
+        turn_z = jnp.where(z >= HALF, 1, cells[1] - 1)
+        abs_y, abs_z = jnp.abs(xi_y), jnp.abs(xi_z)
+        stay = 1.0 - (abs_y * coef[sign_y, 1, 0] + abs_z * coef[sign_z, 2, 0])
+        in_y = abs_y * coef[sign_y, 1, 1]
+        in_z = abs_z * coef[sign_z, 2, 1]
+        out_x, in_x = coef[half, 0, 0], coef[half, 0, 1]
+        extra = row(xi_y, xi_z) if row else None
+        for i in range(HALF):
+            ix = half * HALF + i
+            f = source[j, ix]
+            value = (
+                f * (stay - abs_of[i] * out_x)
+                + in_y * rolled(f, turn_y, 0)
+                + in_z * rolled(f, turn_z, 1)
+                + abs_of[i] * (in_x * halo[j, ix])
+            )
+            store(j, ix, value, extra)
+        return carry
+
+    lax.fori_loop(0, size, one, 0, unroll=math.gcd(4, size))
+
+
+def fill_bells(gx, near):
+    u, per_temp, s = near[0], near[3], near[4]
+
+    def one(i, _):
+        c = speed_of(i) - u
+        part = c * c * per_temp
+        gx[0, i] = jnp.exp(-0.5 * part)
+        gx[1, i] = s * c
+        gx[2, i] = part
+        return 0
+
+    lax.fori_loop(0, NQ, one, 0, unroll=4)
+
+
+def bell_row(near, xi_y, xi_z):
+    c_y, c_z = xi_y - near[1], xi_z - near[2]
+    part = (c_y * c_y + c_z * c_z) * near[3]
+    return jnp.exp(-0.5 * part) * near[8], near[5] * c_y + near[6] * c_z, part - 5.0
+
+
+def relaxed(gx, near, ix, value, extra):
+    height, along, part = extra
+    return value * near[7] + gx[0, ix] * height * (1.0 + (gx[1, ix] + along) * (gx[2, ix] + part))
+
+
+def last_kernel(rows, base_ref, halo_ref, state_ref, coef_ref, out_ref, gx):
+    rank, piece = lax.axis_index("vel"), pl.program_id(0)
+    size = base_ref.shape[0]
+    near = [state_ref[k] for k in range(9)]
+
+    @pl.when(piece == 0)
+    def _():
+        fill_bells(gx, near)
+
+    def speeds(j):
+        row = rank * rows + piece * size + j
+        return lax.rem(row, NQ), lax.div(row, NQ)
+
+    def store(j, ix, value, extra):
+        out_ref[j, ix] = relaxed(gx, near, ix, value, extra)
+
+    for half in range(2):
+        upwind(base_ref, halo_ref, coef_ref, half, speeds, size, store, functools.partial(bell_row, near))
+
+
 def kernel(
-    n_slab, n_vel, f_ref, links_ref, solid_ref, out_ref,
-    f0, base, last, halo0, halo1, links_all, solid_all, send1, send2, gather_in, all1, all2,
+    n_slab, n_vel, f_ref, links_ref, solid_ref, base_out, halo1, state_out, coef_out,
+    f0, base, halo0, state, links_all, solid_all, send1, send2, gather_in, all1, all2,
     faces, coef, gx, pred,
-    load_sem, link_sem, link_send, halo_recv, halo_send, rs_recv, rs_send, ag_recv, ag_send, out_sem,
+    load_sem, link_sem, link_send, halo_recv, halo_send, rs_recv, rs_send, ag_recv, ag_send, out_sem, zero_sem,
 ):
     slab = lax.axis_index("slab")
     rank = lax.axis_index("vel")
@@ -189,10 +266,14 @@
             for i in range(HALF):
                 zero = jnp.zeros(f0.shape[2:], jnp.float32)
                 halo0[j, low + i] = zero
-                halo1[j, low + i] = zero
             return 0
 
         lax.fori_loop(0, rows, one, 0)
+        zero_copy(low).start()
+
+    def zero_copy(low):
+        where = (slice(None), pl.ds(low, HALF))
+        return pltpu.make_async_copy(halo0.at[where], halo1.at[where], zero_sem.at[low // HALF])
 
     @pl.when(jnp.logical_not(has_below))
     def _():
@@ -343,70 +424,10 @@
         coef[1, a, 0] = pred[2, slab]
         coef[1, a, 1] = pred[0, slab]
 
-    def streamed(source, halo, half, first_row, row_end, finish):
-        cells = f0.shape[2:]
-        abs_of = [jnp.abs(speed_of(half * HALF + i)) for i in range(HALF)]
-
-        def one(j, carry):
-            y, z = row_speeds(j)
-            xi_y, xi_z = speed_of(y), speed_of(z)
-            sign_y = jnp.where(y >= HALF, 1, 0)
-            sign_z = jnp.where(z >= HALF, 1, 0)
-            turn_y = jnp.where(y >= HALF, 1, cells[0] - 1)
-            turn_z = jnp.where(z >= HALF, 1, cells[1] - 1)
-            abs_y, abs_z = jnp.abs(xi_y), jnp.abs(xi_z)
-            stay = 1.0 - (abs_y * coef[sign_y, 1, 0] + abs_z * coef[sign_z, 2, 0])
-            in_y = abs_y * coef[sign_y, 1, 1]
-            in_z = abs_z * coef[sign_z, 2, 1]
-            out_x, in_x = coef[half, 0, 0], coef[half, 0, 1]
-            extra = finish.row(j, xi_y, xi_z) if finish else None
-            for i in range(HALF):
-                ix = half * HALF + i
-                abs_x = abs_of[i]
-                f = source[j, ix]
-                value = (
-                    f * (stay - abs_x * out_x)
-                    + in_y * rolled(f, turn_y, 0)
-                    + in_z * rolled(f, turn_z, 1)
-                    + abs_x * (in_x * halo[j, ix])
-                )
-                if finish:
-                    finish.store(j, ix, value, extra)
-                else:
-                    base[j, ix] = value
-            return carry
-
-        lax.fori_loop(first_row, row_end, one, 0, unroll=math.gcd(4, row_end - first_row))
-
-    class Goal:
-        def __init__(self, target, u, per_temp, s, inv, amp):
-            self.target, self.u, self.per_temp, self.s, self.inv, self.amp = target, u, per_temp, s, inv, amp
-
-            def one(i, _):
-                c = speed_of(i) - u[0]
-                part = c * c * per_temp
-                gx[0, i] = jnp.exp(-0.5 * part)
-                gx[1, i] = s[0] * c
-                gx[2, i] = part
-                return 0
-
-            lax.fori_loop(0, NQ, one, 0, unroll=4)
-
-        def row(self, j, xi_y, xi_z):
-            c_y, c_z = xi_y - self.u[1], xi_z - self.u[2]
-            part = (c_y * c_y + c_z * c_z) * self.per_temp
-            return jnp.exp(-0.5 * part) * self.amp, self.s[1] * c_y + self.s[2] * c_z, part - 5.0
-
-        def store(self, j, ix, value, extra):
-            height, along, part = extra
-            bell = gx[0, ix] * height
-            self.target[j, ix] = value * self.inv + bell * (1.0 + (gx[1, ix] + along) * (gx[2, ix] + part))
+    coef_copy = pltpu.make_async_copy(coef, coef_out, out_sem.at[1])
+    coef_copy.start()
 
     lead = jnp.where(has_above, 1, 0)
-
-    def both_halves(body):
-        for turn in range(2):
-            body(lead if turn == 0 else 1 - lead, turn)
 
     def wait_dynamic(source, halo, which, half):
         @pl.when(half == 1)
@@ -454,7 +475,11 @@
 
     def first_pass(half, turn):
         wait_dynamic(f0, halo0, 0, half)
-        streamed(f0, halo0, half, 0, rows, None)
+
+        def store(j, ix, value, extra):
+            base[j, ix] = value
+
+        upwind(f0, halo0, coef, half, row_speeds, rows, store)
 
     first_pass(lead, 0)
 
@@ -492,16 +517,16 @@
             pred[k] = plane
         return [pred[k, slab] for k in range(len(planes))]
 
-    near = own([*u, per_temp, *s, inv])
-    near_amp = own([amp])[0]
-    goal = Goal(base, near[0:3], near[3], near[4:7], near[7], near_amp)
+    near = own([*u, per_temp, *s, inv]) + own([amp])
+    fill_bells(gx, near)
 
     def relax_rows(half):
         def one(j, carry):
             y, z = row_speeds(j)
-            extra = goal.row(j, speed_of(y), speed_of(z))
+            extra = bell_row(near, speed_of(y), speed_of(z))
             for i in range(HALF):
-                goal.store(j, half * HALF + i, base[j, half * HALF + i], extra)
+                ix = half * HALF + i
+                base[j, ix] = relaxed(gx, near, ix, base[j, ix], extra)
             return carry
 
         lax.fori_loop(0, rows, one, 0, unroll=math.gcd(4, rows))
@@ -521,6 +546,8 @@
             halo_copy(base, halo1, 1, 0).start()
 
     relax_rows(1 - lead)
+    base_copy = pltpu.make_async_copy(base, base_out, out_sem.at[0])
+    base_copy.start()
 
     @pl.when(jnp.logical_and(lead == 1, has_below))
     def _():
@@ -533,23 +560,17 @@
         predict(all2[k * n_slab:(k + 1) * n_slab] * inv + target[k]) for k in range(MOMENTS)
     ]
     u, per_temp, s, inv, amp = masked_state(state2, solid)
-    near = own([*u, per_temp, *s, inv])
-    near_amp = own([amp])[0]
-    final = Goal(last, near[0:3], near[3], near[4:7], near[7], near_amp)
-
-    stores = []
-
-    def last_pass(half, turn):
-        wait_dynamic(base, halo1, 1, half)
-        cut = rows // 2
-        for piece in range(2):
-            streamed(base, halo1, half, piece * cut, (piece + 1) * cut, final)
-            where = (pl.ds(piece * cut, cut), pl.ds(half * HALF, HALF))
-            copy = pltpu.make_async_copy(last.at[where], out_ref.at[where], out_sem.at[turn, piece])
-            copy.start()
-            stores.append(copy)
-
-    both_halves(last_pass)
+    for k, plane in enumerate(own([*u, per_temp, *s, inv]) + own([amp])):
+        state[k] = plane
+    state_copy = pltpu.make_async_copy(state, state_out, out_sem.at[2])
+    state_copy.start()
+
+    for half in range(2):
+        wait_halo(base, halo1, 1, half)
+
+        @pl.when(jnp.logical_not(has_below if half else has_above))
+        def _():
+            zero_copy(half * HALF).wait()
 
     wait_halo_send(f0, halo0, 0)
     wait_halo_send(base, halo1, 1)
@@ -571,7 +592,7 @@
         def _():
             pltpu.make_async_copy(source, source, rs_send.at[which]).wait()
 
-    for copy in stores:
+    for copy in (base_copy, coef_copy, state_copy):
         copy.wait()
 
 
@@ -585,13 +606,16 @@
     block = (rows, NQ) + cells
     grid = (n_slab,) + cells
     any_spec = pl.BlockSpec(memory_space=pltpu.HBM)
-    out = pl.pallas_call(
+    base, halo, state, coef = pl.pallas_call(
         functools.partial(kernel, n_slab, n_vel),
-        out_shape=jax.ShapeDtypeStruct(block, f32),
+        out_shape=[
+            jax.ShapeDtypeStruct(block, f32), jax.ShapeDtypeStruct(block, f32),
+            jax.ShapeDtypeStruct((9,) + cells, f32), jax.ShapeDtypeStruct((2, 3, 2) + cells, f32),
+        ],
         in_specs=[any_spec] * 3,
-        out_specs=any_spec,
+        out_specs=[any_spec] * 4,
         scratch_shapes=[
-            vmem(block, f32), vmem(block, f32), vmem(block, f32), vmem(block, f32), vmem(block, f32),
+            vmem(block, f32), vmem(block, f32), vmem(block, f32), vmem((9,) + cells, f32),
             vmem((n_slab, 3) + cells, jnp.int32), vmem(grid, jnp.int32),
             vmem((MOMENTS,) + cells, f32), vmem((MOMENTS,) + cells, f32),
             vmem((n_vel,) + cells, f32),
@@ -599,12 +623,27 @@
             vmem((7,) + grid, f32), vmem((2, 3, 2) + cells, f32), vmem((3, NQ) + cells, f32),
             vmem((MOMENTS,) + grid, f32),
             dma((3,)), dma((2,)), dma((2, n_slab)), dma((2, 2)), dma((2, 2)), dma, dma((2,)),
-            dma((2,)), dma((n_slab,)), dma((2, 2)),
+            dma((2,)), dma((n_slab,)), dma((3,)), dma((2,)),
         ],
         compiler_params=pltpu.CompilerParams(
             collective_id=0, has_side_effects=True, vmem_limit_bytes=60 * 1024 * 1024
         ),
     )(f_start.reshape(block), links.reshape((3,) + cells), solid.reshape(cells))
+    pieces = math.gcd(4, rows)
+    piece = pl.BlockSpec((rows // pieces, NQ) + cells, lambda i: (i, 0, 0, 0))
+    out = pl.pallas_call(
+        functools.partial(last_kernel, rows),
+        grid=(pieces,),
+        out_shape=jax.ShapeDtypeStruct(block, f32),
+        in_specs=[
+            piece, piece,
+            pl.BlockSpec((9,) + cells, lambda i: (0, 0, 0)),
+            pl.BlockSpec((2, 3, 2) + cells, lambda i: (0, 0, 0, 0, 0)),
+        ],
+        out_specs=piece,
+        scratch_shapes=[vmem((3, NQ) + cells, f32)],
+        compiler_params=pltpu.CompilerParams(vmem_limit_bytes=60 * 1024 * 1024),
+    )(base, halo, state, coef)
     return out.reshape(f_start.shape)
 
 

time: 23.3 us -> 23.9 us (1.026)
  Pallas kernels: 20.8 us -> 23.6 us
  local copies, waits for them, and re-layouts: 2.26 us -> 0 us
    pallas_call x1 -> x2, Pallas kernels: 20.8 us -> 23.6 us  [the longest x1 19.6 us: body(): pl.pallas_call(functools.partial(kernel, n_slab, n_vel), out_shape=[jax.S...]
    unnamed x1 -> x0, local copies, waits for them, and re-layouts: 2.26 us -> none
where the time goes in v4:
time: 23.9 us; the launch traced here: 23.6 us
  Pallas kernels  23.6 us (99%)
    pallas_call x1, Pallas kernels, body(): pl.pallas_call(functools.partial(kernel, n_slab, n_vel), out_shape=[jax.S...  19.6 us
    pallas_call x1, Pallas kernels, body(): pl.pallas_call(functools.partial(last_kernel, rows), grid=(pieces,), out_...  3.99 us

profile of v4, /device:TPU:1, one launch (start us, length us, event | category | flops | bytes accessed | tf_op | source)
XLA Modules:
  0.0 23.6 jit_solution(17338580647144048)
XLA Ops:
  0.0 19.6 %shard_map.37 = (f32[16,16,8,128]{3,2,1,0:T(8,128)}, f32[16,16,8,128]{3,2,1,0:T(8,128)}, f32[9,8,128]{2,1,0:T(8,128)}, f32[2,3,2,8,128]{4,3,2,1,0:T(8,128)}) custom-call(f32[16,16,8,128]{3,2,1,0:T(8,128)} %bitcast.6, s32[3,8,128]{2,1,0:T(8,128)} %bitcast.7, s32[8,128]{1,0:T(8,128)} %bitcast.8), custom_call_target="tpu_custom_call" | custom-call | tf_op jit(solution)/shard_map/pallas_call | solution.py:609
  19.7 4.0 %shard_map.38 = f32[16,16,8,128]{3,2,1,0:T(8,128)} custom-call(f32[16,16,8,128]{3,2,1,0:T(8,128)} %get-tuple-element.9.base_ref, f32[16,16,8,128]{3,2,1,0:T(8,128)} %get-tuple-element.10.halo_ref, f32[9,8,128]{2,1,0:T(8,128)} %get-tuple-element.11.state_ref, f32[2,3,2,8,128]{4,3,2,1,0:T(8,128)} %get-tuple-element.12.coef_ref), custom_call_target="tpu_custom_call" | custom-call | tf_op jit(solution)/shard_map/pallas_call | solution.py:634

commit v5 on v3

--- a/solution.py
+++ b/solution.py
@@ -144,9 +144,9 @@
 
 def kernel(
     n_slab, n_vel, f_ref, links_ref, solid_ref, out_ref,
-    f0, base, last, halo0, halo1, links_all, solid_all, send1, send2, gather_in, all1, all2,
+    f0, base, halo0, halo1, links_all, solid_all, send1, send2, gather_in, all1, all2,
     faces, coef, gx, pred,
-    load_sem, link_sem, link_send, halo_recv, halo_send, rs_recv, rs_send, ag_recv, ag_send, out_sem,
+    load_sem, link_sem, link_send, halo_recv, halo_send, rs_recv, rs_send, ag_recv, ag_send,
 ):
     slab = lax.axis_index("slab")
     rank = lax.axis_index("vel")
@@ -535,19 +535,11 @@
     u, per_temp, s, inv, amp = masked_state(state2, solid)
     near = own([*u, per_temp, *s, inv])
     near_amp = own([amp])[0]
-    final = Goal(last, near[0:3], near[3], near[4:7], near[7], near_amp)
-
-    stores = []
+    final = Goal(out_ref, near[0:3], near[3], near[4:7], near[7], near_amp)
 
     def last_pass(half, turn):
         wait_dynamic(base, halo1, 1, half)
-        cut = rows // 2
-        for piece in range(2):
-            streamed(base, halo1, half, piece * cut, (piece + 1) * cut, final)
-            where = (pl.ds(piece * cut, cut), pl.ds(half * HALF, HALF))
-            copy = pltpu.make_async_copy(last.at[where], out_ref.at[where], out_sem.at[turn, piece])
-            copy.start()
-            stores.append(copy)
+        streamed(base, halo1, half, 0, rows, final)
 
     both_halves(last_pass)
 
@@ -570,9 +562,6 @@
         @pl.when(jnp.logical_not(reduces))
         def _():
             pltpu.make_async_copy(source, source, rs_send.at[which]).wait()
-
-    for copy in stores:
-        copy.wait()
 
 
 def body(f_start, links, solid):
@@ -589,9 +578,9 @@
         functools.partial(kernel, n_slab, n_vel),
         out_shape=jax.ShapeDtypeStruct(block, f32),
         in_specs=[any_spec] * 3,
-        out_specs=any_spec,
+        out_specs=pl.BlockSpec(memory_space=pltpu.VMEM),
         scratch_shapes=[
-            vmem(block, f32), vmem(block, f32), vmem(block, f32), vmem(block, f32), vmem(block, f32),
+            vmem(block, f32), vmem(block, f32), vmem(block, f32), vmem(block, f32),
             vmem((n_slab, 3) + cells, jnp.int32), vmem(grid, jnp.int32),
             vmem((MOMENTS,) + cells, f32), vmem((MOMENTS,) + cells, f32),
             vmem((n_vel,) + cells, f32),
@@ -599,12 +588,15 @@
             vmem((7,) + grid, f32), vmem((2, 3, 2) + cells, f32), vmem((3, NQ) + cells, f32),
             vmem((MOMENTS,) + grid, f32),
             dma((3,)), dma((2,)), dma((2, n_slab)), dma((2, 2)), dma((2, 2)), dma, dma((2,)),
-            dma((2,)), dma((n_slab,)), dma((2, 2)),
+            dma((2,)), dma((n_slab,)),
         ],
         compiler_params=pltpu.CompilerParams(
-            collective_id=0, has_side_effects=True, vmem_limit_bytes=60 * 1024 * 1024
+            collective_id=0, has_side_effects=True, vmem_limit_bytes=32 * 1024 * 1024
         ),
-    )(f_start.reshape(block), links.reshape((3,) + cells), solid.reshape(cells))
+    )(*(
+        pltpu.with_memory_space_constraint(x, pltpu.HBM)
+        for x in (f_start.reshape(block), links.reshape((3,) + cells), solid.reshape(cells))
+    ))
     return out.reshape(f_start.shape)
 
 

time: 23.3 us -> 21.3 us (0.914)
  local copies, waits for them, and re-layouts: 2.26 us -> 0.97 us
  Pallas kernels: 20.8 us -> 20 us
    unnamed x1, local copies, waits for them, and re-layouts: 2.26 us -> 0.97 us
    pallas_call x1, Pallas kernels: 20.8 us -> 20 us  [body(): pl.pallas_call(functools.partial(kernel, n_slab, n_vel), out_shape=jax.Sh...]
where the time goes in v5:
time: 21.3 us; the launch traced here: 21 us
  Pallas kernels  20 us (94%)
  local copies, waits for them, and re-layouts  0.97 us (5%)
    pallas_call x1, Pallas kernels, body(): pl.pallas_call(functools.partial(kernel, n_slab, n_vel), out_shape=jax.Sh...  20 us
    unnamed x1, local copies, waits for them, and re-layouts  0.97 us

profile of v5, /device:TPU:1, one launch (start us, length us, event | category | flops | bytes accessed | tf_op | source)
XLA Modules:
  0.0 21.0 jit_solution(4199243813629547633)
XLA Ops:
  0.0 20.0 %shard_map.37 = f32[16,16,8,128]{3,2,1,0:T(8,128)S(1)} custom-call(f32[16,16,8,128]{3,2,1,0:T(8,128)} %bitcast.7, s32[3,8,128]{2,1,0:T(8,128)} %bitcast.8, s32[8,128]{1,0:T(8,128)} %bitcast.9), custom_call_target="tpu_custom_call" | custom-call | tf_op jit(solution)/shard_map/pallas_call | solution.py:577
  20.0 1.0 %copy.6 = f32[256,1,8,128]{3,2,1,0:T(8,128)} copy(f32[256,1,8,128]{3,2,1,0:T(8,128)S(1)} %bitcast.6) | data formatting | bytes 2097152

commit v6 on v5

--- a/solution.py
+++ b/solution.py
@@ -146,11 +146,13 @@
     n_slab, n_vel, f_ref, links_ref, solid_ref, out_ref,
     f0, base, halo0, halo1, links_all, solid_all, send1, send2, gather_in, all1, all2,
     faces, coef, gx, pred,
-    load_sem, link_sem, link_send, halo_recv, halo_send, rs_recv, rs_send, ag_recv, ag_send,
+    f_sem, load_sem, link_sem, link_send, halo_recv, halo_send, rs_recv, rs_send, ag_recv, ag_send,
 ):
     slab = lax.axis_index("slab")
     rank = lax.axis_index("vel")
     rows = f_ref.shape[0]
+    chunks = math.gcd(4, rows)
+    size = rows // chunks
     first1 = n_vel // 2 - MOMENTS // 2
     first2 = n_vel // 2 + MOMENTS // 2
     plane1 = rank - first1
@@ -165,11 +167,12 @@
             copy.start()
 
     loads = [
-        pltpu.make_async_copy(f_ref, f0, load_sem.at[0]),
-        pltpu.make_async_copy(links_ref, links_all.at[slab], load_sem.at[1]),
-        pltpu.make_async_copy(solid_ref, solid_all.at[slab], load_sem.at[2]),
+        pltpu.make_async_copy(links_ref, links_all.at[slab], load_sem.at[0]),
+        pltpu.make_async_copy(solid_ref, solid_all.at[slab], load_sem.at[1]),
     ]
-    start_all(loads)
+    pieces = [pl.ds(c * size, size) for c in range(chunks)]
+    f_loads = [pltpu.make_async_copy(f_ref.at[p], f0.at[p], f_sem.at[c]) for c, p in enumerate(pieces)]
+    start_all(f_loads + loads)
 
     barrier = pltpu.get_barrier_semaphore()
     for step in range(n_slab):
@@ -214,7 +217,7 @@
             sums[4] + e, sums[5] + 0.5 * (a3 + r * a1), sums[6] + xi_y * e, sums[7] + xi_z * e,
         )
 
-    def moments_of(source):
+    def moments_of(source, ready=None):
         def one(j, sums):
             y, z = row_speeds(j)
             a0 = a1 = a2 = a3 = None
@@ -231,14 +234,18 @@
             return add_row(sums, a0, a1, a2, a3, speed_of(y), speed_of(z))
 
         zero = jnp.zeros(f0.shape[2:], jnp.float32)
-        return lax.fori_loop(0, rows, one, (zero,) * MOMENTS, unroll=2)
-
-    loads[0].wait()
-    m1 = moments_of(f0)
+        sums = (zero,) * MOMENTS
+        for c in range(chunks):
+            if ready:
+                ready[c].wait()
+            sums = lax.fori_loop(c * size, (c + 1) * size, one, sums, unroll=math.gcd(2, size))
+        return sums
+
+    m1 = moments_of(f0, f_loads)
     for k in range(MOMENTS):
         send1[k] = m1[k]
+    loads[0].wait()
     loads[1].wait()
-    loads[2].wait()
     pl.semaphore_wait(barrier, n_slab * n_vel - 1)
 
     def scatter(source, first):
@@ -273,39 +280,35 @@
 
     up_half, low_half = pl.ds(HALF, HALF), pl.ds(0, HALF)
 
-    def halo_copy(source, halo, which, half):
+    def halo_copy(source, halo, which, half, c):
         part = up_half if half else low_half
         to_slab = slab + 1 if half else slab - 1
         return pltpu.make_async_remote_copy(
-            src_ref=source.at[:, part], dst_ref=halo.at[:, part],
-            send_sem=halo_send.at[which, half], recv_sem=halo_recv.at[which, half],
+            src_ref=source.at[pieces[c], part], dst_ref=halo.at[pieces[c], part],
+            send_sem=halo_send.at[which, half, c], recv_sem=halo_recv.at[which, half, c],
             device_id={"slab": to_slab}, device_id_type=MESH,
         )
 
-    def send_halo(source, halo, which):
-        @pl.when(has_above)
-        def _():
-            halo_copy(source, halo, which, 1).start()
-
-        @pl.when(has_below)
-        def _():
-            halo_copy(source, halo, which, 0).start()
-
-    def wait_halo(source, halo, which, half):
+    def send_halo(source, halo, which, half, c):
+        @pl.when(has_above if half else has_below)
+        def _():
+            halo_copy(source, halo, which, half, c).start()
+
+    def wait_halo(source, halo, which, half, c):
         @pl.when(has_below if half else has_above)
         def _():
-            halo_copy(source, halo, which, half).wait_recv()
+            halo_copy(source, halo, which, half, c).wait_recv()
 
     def wait_halo_send(source, halo, which):
-        @pl.when(has_above)
-        def _():
-            halo_copy(source, halo, which, 1).wait_send()
-
-        @pl.when(has_below)
-        def _():
-            halo_copy(source, halo, which, 0).wait_send()
-
-    send_halo(f0, halo0, 0)
+        for half in range(2):
+            @pl.when(has_above if half else has_below)
+            def _():
+                for c in range(chunks):
+                    halo_copy(source, halo, which, half, c).wait_send()
+
+    for c in range(chunks):
+        send_halo(f0, halo0, 0, 1, c)
+        send_halo(f0, halo0, 0, 0, c)
 
     if n_slab > 1:
         others = pl.ds(0, n_slab - 1)
@@ -408,14 +411,14 @@
         for turn in range(2):
             body(lead if turn == 0 else 1 - lead, turn)
 
-    def wait_dynamic(source, halo, which, half):
+    def wait_dynamic(source, halo, which, half, c):
         @pl.when(half == 1)
         def _():
-            wait_halo(source, halo, which, 1)
+            wait_halo(source, halo, which, 1, c)
 
         @pl.when(half == 0)
         def _():
-            wait_halo(source, halo, which, 0)
+            wait_halo(source, halo, which, 0, c)
 
     def reduce_and_send(plane, source, everything, which):
         pltpu.make_async_copy(
@@ -453,8 +456,9 @@
             pltpu.make_async_copy(everything, everything, ag_recv.at[which]).wait()
 
     def first_pass(half, turn):
-        wait_dynamic(f0, halo0, 0, half)
-        streamed(f0, halo0, half, 0, rows, None)
+        for c in range(chunks):
+            wait_dynamic(f0, halo0, 0, half, c)
+            streamed(f0, halo0, half, c * size, (c + 1) * size, None)
 
     first_pass(lead, 0)
 
@@ -504,27 +508,16 @@
                 goal.store(j, half * HALF + i, base[j, half * HALF + i], extra)
             return carry
 
-        lax.fori_loop(0, rows, one, 0, unroll=math.gcd(4, rows))
+        for c in range(chunks):
+            lax.fori_loop(c * size, (c + 1) * size, one, 0, unroll=math.gcd(4, size))
+            for side in range(2):
+                @pl.when(half == side)
+                def _(side=side):
+                    send_halo(base, halo1, 1, side, c)
 
     relax_rows(lead)
 
-    @pl.when(lead == 1)
-    def _():
-        @pl.when(has_above)
-        def _():
-            halo_copy(base, halo1, 1, 1).start()
-
-    @pl.when(lead == 0)
-    def _():
-        @pl.when(has_below)
-        def _():
-            halo_copy(base, halo1, 1, 0).start()
-
     relax_rows(1 - lead)
-
-    @pl.when(jnp.logical_and(lead == 1, has_below))
-    def _():
-        halo_copy(base, halo1, 1, 0).start()
 
     target = goal_moments(u, per_temp, s, amp)
 
@@ -538,8 +531,9 @@
     final = Goal(out_ref, near[0:3], near[3], near[4:7], near[7], near_amp)
 
     def last_pass(half, turn):
-        wait_dynamic(base, halo1, 1, half)
-        streamed(base, halo1, half, 0, rows, final)
+        for c in range(chunks):
+            wait_dynamic(base, halo1, 1, half, c)
+            streamed(base, halo1, half, c * size, (c + 1) * size, final)
 
     both_halves(last_pass)
 
@@ -571,6 +565,7 @@
     rows = vel_local // NQ
     assert planes == 1 and rows * NQ == vel_local and rows % 2 == 0 and n_vel >= 2 * MOMENTS
     f32, vmem, dma = jnp.float32, pltpu.VMEM, pltpu.SemaphoreType.DMA
+    chunks = math.gcd(4, rows)
     block = (rows, NQ) + cells
     grid = (n_slab,) + cells
     any_spec = pl.BlockSpec(memory_space=pltpu.HBM)
@@ -587,7 +582,7 @@
             vmem((MOMENTS * n_slab,) + cells, f32), vmem((MOMENTS * n_slab,) + cells, f32),
             vmem((7,) + grid, f32), vmem((2, 3, 2) + cells, f32), vmem((3, NQ) + cells, f32),
             vmem((MOMENTS,) + grid, f32),
-            dma((3,)), dma((2,)), dma((2, n_slab)), dma((2, 2)), dma((2, 2)), dma, dma((2,)),
+            dma((chunks,)), dma((2,)), dma((2,)), dma((2, n_slab)), dma((2, 2, chunks)), dma((2, 2, chunks)), dma, dma((2,)),
             dma((2,)), dma((n_slab,)),
         ],
         compiler_params=pltpu.CompilerParams(

time: 21.3 us -> 21.2 us (level)
  no operation moved by 1% of the time
where the time goes in v6:
time: 21.2 us; the launch traced here: 21 us
  Pallas kernels  20 us (94%)
  local copies, waits for them, and re-layouts  0.97 us (5%)
    pallas_call x1, Pallas kernels, body(): pl.pallas_call(functools.partial(kernel, n_slab, n_vel), out_shape=jax.Sh...  20 us
    unnamed x1, local copies, waits for them, and re-layouts  0.97 us

profile of v6, /device:TPU:1, one launch (start us, length us, event | category | flops | bytes accessed | tf_op | source)
XLA Modules:
  0.0 21.0 jit_solution(9226463459073368346)
XLA Ops:
  0.0 20.0 %shard_map.37 = f32[16,16,8,128]{3,2,1,0:T(8,128)S(1)} custom-call(f32[16,16,8,128]{3,2,1,0:T(8,128)} %bitcast.7, s32[3,8,128]{2,1,0:T(8,128)} %bitcast.8, s32[8,128]{1,0:T(8,128)} %bitcast.9), custom_call_target="tpu_custom_call" | custom-call | tf_op jit(solution)/shard_map/pallas_call | solution.py:572
  20.0 1.0 %copy.6 = f32[256,1,8,128]{3,2,1,0:T(8,128)} copy(f32[256,1,8,128]{3,2,1,0:T(8,128)S(1)} %bitcast.6) | data formatting | bytes 2097152

commit v7 on v5

--- a/solution.py
+++ b/solution.py
@@ -146,7 +146,7 @@
     n_slab, n_vel, f_ref, links_ref, solid_ref, out_ref,
     f0, base, halo0, halo1, links_all, solid_all, send1, send2, gather_in, all1, all2,
     faces, coef, gx, pred,
-    load_sem, link_sem, link_send, halo_recv, halo_send, rs_recv, rs_send, ag_recv, ag_send,
+    load_sem, link_sem, link_send, halo_recv, halo_send, rs_recv, rs_send, ag_recv, ag_send, fwd_recv, fwd_send,
 ):
     slab = lax.axis_index("slab")
     rank = lax.axis_index("vel")
@@ -425,32 +425,42 @@
         total = gather_in[0]
         for v in range(1, n_vel):
             total = total + gather_in[v]
-        mine = plane * n_slab + slab
+        mine = slab * MOMENTS + plane
         everything[mine] = total
-        for step in range(n_slab):
-            to_slab = lax.rem(slab + step, n_slab)
-
-            def one(i, _, to_slab=to_slab, step=step):
-                pltpu.make_async_remote_copy(
-                    src_ref=everything.at[mine], dst_ref=everything.at[mine],
-                    send_sem=ag_send.at[step], recv_sem=ag_recv.at[which],
-                    device_id={"slab": to_slab, "vel": lax.rem(rank + i, n_vel)}, device_id_type=MESH,
-                ).start()
-                return 0
-
-            lax.fori_loop(1 if step == 0 else 0, n_vel, one, 0, unroll=5 if step == 0 else 4)
+        def one(i, _):
+            pltpu.make_async_remote_copy(
+                src_ref=everything.at[mine], dst_ref=everything.at[mine],
+                send_sem=ag_send.at[0], recv_sem=ag_recv.at[which],
+                device_id={"vel": lax.rem(rank + i, n_vel)}, device_id_type=MESH,
+            ).start()
+            return 0
+
+        lax.fori_loop(1, n_vel, one, 0, unroll=5)
 
     def wait_gathered(everything, which, reduces):
-        planes = MOMENTS * n_slab
-
         @pl.when(reduces)
         def _():
-            part = everything.at[pl.ds(0, planes - 1)]
+            part = everything.at[pl.ds(0, MOMENTS - 1)]
             pltpu.make_async_copy(part, part, ag_recv.at[which]).wait()
 
         @pl.when(jnp.logical_not(reduces))
         def _():
-            pltpu.make_async_copy(everything, everything, ag_recv.at[which]).wait()
+            part = everything.at[pl.ds(0, MOMENTS)]
+            pltpu.make_async_copy(part, part, ag_recv.at[which]).wait()
+
+        own_sums = everything.at[pl.ds(slab * MOMENTS, MOMENTS)]
+        for step in range(1, n_slab):
+            pltpu.make_async_remote_copy(
+                src_ref=own_sums, dst_ref=own_sums, send_sem=fwd_send.at[which, step],
+                recv_sem=fwd_recv.at[which], device_id={"slab": lax.rem(slab + step, n_slab)},
+                device_id_type=MESH,
+            ).start()
+        if n_slab > 1:
+            part = everything.at[pl.ds(0, MOMENTS * (n_slab - 1))]
+            pltpu.make_async_copy(part, part, fwd_recv.at[which]).wait()
+
+    def over_slabs(everything, k):
+        return jnp.stack([everything[p * MOMENTS + k] for p in range(n_slab)])
 
     def first_pass(half, turn):
         wait_dynamic(f0, halo0, 0, half)
@@ -484,7 +494,7 @@
         reduce_and_send(plane2, send2, all2, 1)
 
     wait_gathered(all1, 0, reduces1)
-    state1 = [predict(all1[k * n_slab:(k + 1) * n_slab]) for k in range(MOMENTS)]
+    state1 = [predict(over_slabs(all1, k)) for k in range(MOMENTS)]
     u, per_temp, s, inv, amp = masked_state(state1, solid)
 
     def own(planes):
@@ -530,7 +540,7 @@
 
     wait_gathered(all2, 1, reduces2)
     state2 = [
-        predict(all2[k * n_slab:(k + 1) * n_slab] * inv + target[k]) for k in range(MOMENTS)
+        predict(over_slabs(all2, k) * inv + target[k]) for k in range(MOMENTS)
     ]
     u, per_temp, s, inv, amp = masked_state(state2, solid)
     near = own([*u, per_temp, *s, inv])
@@ -549,15 +559,16 @@
         pltpu.make_async_copy(links_all.at[0], links_all.at[0], link_send.at[0, step]).wait()
         pltpu.make_async_copy(solid_all.at[0], solid_all.at[0], link_send.at[1, step]).wait()
     for which, reduces in ((0, reduces1), (1, reduces2)):
+        for step in range(1, n_slab):
+            pltpu.make_async_copy(send1, send1, fwd_send.at[which, step]).wait()
         source = send1 if which == 0 else send2
 
         @pl.when(reduces)
         def _():
             part = source.at[pl.ds(0, MOMENTS - 1)]
             pltpu.make_async_copy(part, part, rs_send.at[which]).wait()
-            for step in range(n_slab):
-                part = gather_in.at[pl.ds(0, n_vel - 1 if step == 0 else n_vel)]
-                pltpu.make_async_copy(part, part, ag_send.at[step]).wait()
+            part = gather_in.at[pl.ds(0, n_vel - 1)]
+            pltpu.make_async_copy(part, part, ag_send.at[0]).wait()
 
         @pl.when(jnp.logical_not(reduces))
         def _():
@@ -588,7 +599,7 @@
             vmem((7,) + grid, f32), vmem((2, 3, 2) + cells, f32), vmem((3, NQ) + cells, f32),
             vmem((MOMENTS,) + grid, f32),
             dma((3,)), dma((2,)), dma((2, n_slab)), dma((2, 2)), dma((2, 2)), dma, dma((2,)),
-            dma((2,)), dma((n_slab,)),
+            dma((2,)), dma((1,)), dma((2,)), dma((2, n_slab)),
         ],
         compiler_params=pltpu.CompilerParams(
             collective_id=0, has_side_effects=True, vmem_limit_bytes=32 * 1024 * 1024

time: 21.3 us -> 22 us (1.033)
  Pallas kernels: 20 us -> 20.9 us
    pallas_call x1, Pallas kernels: 20 us -> 20.9 us  [body(): pl.pallas_call(functools.partial(kernel, n_slab, n_vel), out_shape=jax.Sh...]
where the time goes in v7:
time: 22 us; the launch traced here: 21.9 us
  Pallas kernels  20.9 us (95%)
  local copies, waits for them, and re-layouts  0.97 us (4%)
    pallas_call x1, Pallas kernels, body(): pl.pallas_call(functools.partial(kernel, n_slab, n_vel), out_shape=jax.Sh...  20.9 us
    unnamed x1, local copies, waits for them, and re-layouts  0.97 us

profile of v7, /device:TPU:1, one launch (start us, length us, event | category | flops | bytes accessed | tf_op | source)
XLA Modules:
  0.0 21.9 jit_solution(5837484848530147368)
XLA Ops:
  0.0 20.9 %shard_map.37 = f32[16,16,8,128]{3,2,1,0:T(8,128)S(1)} custom-call(f32[16,16,8,128]{3,2,1,0:T(8,128)} %bitcast.7, s32[3,8,128]{2,1,0:T(8,128)} %bitcast.8, s32[8,128]{1,0:T(8,128)} %bitcast.9), custom_call_target="tpu_custom_call" | custom-call | tf_op jit(solution)/shard_map/pallas_call | solution.py:588
  20.9 1.0 %copy.6 = f32[256,1,8,128]{3,2,1,0:T(8,128)} copy(f32[256,1,8,128]{3,2,1,0:T(8,128)S(1)} %bitcast.6) | data formatting | bytes 2097152
